TPU v7x, 512 devices: a whole 4x8x8 slice. The times are simulated.
512 devices in a mesh: dp: 64 (over y, x, core), tensor: 8 (over z).
Axes of the slice: x: 4, y: 8, z: 8, core: 2. Of those that a mesh axis runs over, the one named last changes fastest.
Arguments:
- queries: bfloat16 [2, 8192, 2048], P(None, 'dp', 'tensor'), may hold values from -5 to 5
- key_rows: bfloat16 [2, 8192, 2048], P(None, 'dp', 'tensor'), may hold values from -5 to 5
- value_rows: bfloat16 [2, 8192, 2048], P(None, 'dp', 'tensor'), may hold values from -5 to 5
- out_weight: bfloat16 [2048, 2048], P('tensor'), may hold values from -0.125 to 0.125
- out_grad: bfloat16 [2, 8192, 2048], P(None, 'dp', 'tensor'), may hold values from -16 to 16
- ibd_lists: int32 [2, 64, 9], replicated, may hold values from 0 to 63, as said below
- ibd_counts: int32 [2, 64], replicated, may hold values from 1 to 9, as said below
Outputs:
- layer_out: bfloat16 [2, 8192, 2048], P(None, 'dp', 'tensor')
- query_grad: bfloat16 [2, 8192, 2048], P(None, 'dp', 'tensor')
- key_grad: bfloat16 [2, 8192, 2048], P(None, 'dp', 'tensor')
- value_grad: bfloat16 [2, 8192, 2048], P(None, 'dp', 'tensor')
- proj_grad: float32 [2048, 2048], P('dp', 'tensor')
Inputs may be any that keep to these rules, and one draw needn't show every extreme that they name: The first ibd_counts[v, i] entries of ibd_lists[v, i] are distinct blocks within 4 blocks of i, the first being i itself; later entries repeat i. A block other than i is among the live entries of ibd_lists[v, i] for at most one variant v. ibd_counts[v, i] is at most the number of blocks within 4 blocks of i, i included.
All inputs are finite; a program needn't handle non-finite values.
Results may differ from a plain program's by a relative error of at most 0.017.
Values may be sent and summed in bfloat16 or wider, within the bound.
A program may use at most 64 MiB of HBM per device.

v0:
```python
import math

import jax
import jax.numpy as jnp
from jax import lax
from jax.sharding import PartitionSpec as P

HD = 128
REACH = 4


NEGATIVE = -1e30


def from_behind(block, axis, distance):
    devices = range(lax.axis_size(axis))
    route = [(i - distance, i) for i in devices if i - distance in devices]
    return lax.ppermute(block, axis, route)


def split_heads(source, head_size):
    return source.reshape(source.shape[0], source.shape[1], source.shape[2] // head_size, head_size)


def weights_from(scores, keep_mask):
    highest = jnp.max(jnp.where(keep_mask, scores, NEGATIVE), axis=-1, keepdims=True)
    totals = jnp.sum(jnp.where(keep_mask, jnp.exp(scores - highest), 0.0), axis=-1, keepdims=True)
    log_totals = highest + jnp.log(totals)
    return (jnp.where(keep_mask, jnp.exp(scores - log_totals), 0.0), log_totals[..., 0])


def local(queries, key_rows, value_rows, out_weight, out_grad, ibd_lists, ibd_counts):
    reach_blocks = REACH
    window_span = 2 * reach_blocks + 1
    variants = queries.shape[0]
    block_rows = queries.shape[1]
    local_width = queries.shape[2]
    head_size = HD
    score_scale = 1.0 / math.sqrt(head_size)
    device_index = lax.axis_index("dp")
    padded_lists = jnp.pad(
        ibd_lists, ((0, 0), (reach_blocks, reach_blocks), (0, 0)), constant_values=-1
    )
    padded_counts = jnp.pad(ibd_counts, ((0, 0), (reach_blocks, reach_blocks)))
    slot_index = jnp.arange(ibd_lists.shape[2], dtype=jnp.int32)
    own_list = lax.dynamic_index_in_dim(
        padded_lists, device_index + reach_blocks, 1, keepdims=False
    )
    own_count = lax.dynamic_index_in_dim(
        padded_counts, device_index + reach_blocks, 1, keepdims=False
    )
    targets = device_index + jnp.arange(window_span, dtype=jnp.int32) - reach_blocks
    listed = jnp.any(
        (own_list[:, :, None] == targets[None, None, :])
        & (slot_index[None, :, None] < own_count[:, None, None]),
        axis=1,
    )
    key_keep = jnp.repeat(listed, block_rows, axis=1)[:, None, None, :]
    key_pair = jnp.stack([key_rows, value_rows])
    fetched = []
    for offset in range(window_span):
        stride = reach_blocks - offset
        if offset == reach_blocks:
            fetched.append(key_pair)
        else:
            fetched.append(from_behind(key_pair, "dp", stride))
    window_pair = jnp.concatenate(fetched, axis=2)
    key_heads = split_heads(window_pair[0], head_size)
    value_heads = split_heads(window_pair[1], head_size)
    query_heads = split_heads(queries, head_size)
    scores = (
        jnp.einsum("vqhd,vkhd->vhqk", query_heads, key_heads, preferred_element_type=jnp.float32)
        * score_scale
    )
    prob_rows, log_totals = weights_from(scores, key_keep)
    prob_low = prob_rows.astype(jnp.bfloat16)
    attended = jnp.einsum(
        "vhqk,vkhd->vqhd", prob_low, value_heads, preferred_element_type=jnp.float32
    ).astype(jnp.bfloat16)
    flat_attended = attended.reshape(variants * block_rows, local_width)
    partial_value = jnp.dot(flat_attended, out_weight, preferred_element_type=jnp.float32).reshape(
        variants, block_rows, -1
    )
    layer_out = lax.psum_scatter(
        partial_value.astype(jnp.bfloat16), "tensor", scatter_dimension=2, tiled=True
    )
    grad_full = lax.all_gather(out_grad, "tensor", axis=2, tiled=True)
    flat_grad = grad_full.reshape(variants * block_rows, grad_full.shape[2])
    attended_grad = jnp.dot(flat_grad, out_weight.T, preferred_element_type=jnp.float32).astype(
        jnp.bfloat16
    )
    proj_grad = lax.psum_scatter(
        lax.dot_general(
            flat_grad, flat_attended, (((0,), (0,)), ((), ())), preferred_element_type=jnp.float32
        ),
        "dp",
        scatter_dimension=0,
        tiled=True,
    )
    attended_grad = attended_grad.reshape(variants, block_rows, local_width)
    grad_heads = split_heads(attended_grad, head_size)
    prob_grads = jnp.einsum(
        "vqhd,vkhd->vhqk", grad_heads, value_heads, preferred_element_type=jnp.float32
    )
    deltas = jnp.sum(prob_rows * prob_grads, axis=-1)
    score_grads = (prob_rows * (prob_grads - deltas[..., None]) * score_scale).astype(jnp.bfloat16)
    query_grad = jnp.einsum(
        "vhqk,vkhd->vqhd", score_grads, key_heads, preferred_element_type=jnp.float32
    )
    query_grad = query_grad.astype(jnp.bfloat16).reshape(queries.shape)
    value_terms = jnp.einsum(
        "vhqk,vqhd->vkhd", prob_low, grad_heads, preferred_element_type=jnp.float32
    )
    key_terms = jnp.einsum(
        "vhqk,vqhd->vkhd", score_grads, query_heads, preferred_element_type=jnp.float32
    )
    grad_terms = jnp.stack([key_terms, value_terms]).reshape(
        2, variants, window_span, block_rows, local_width
    )
    totals = grad_terms[:, :, reach_blocks]
    for offset in range(window_span):
        if offset != reach_blocks:
            stride = offset - reach_blocks
            totals = totals + from_behind(
                grad_terms[:, :, offset].astype(jnp.bfloat16), "dp", stride
            ).astype(jnp.float32)
    key_grad = totals[0].astype(jnp.bfloat16)
    value_grad = totals[1].astype(jnp.bfloat16)
    return (layer_out, query_grad, key_grad, value_grad, proj_grad)


def solution(mesh):
    return jax.shard_map(
        local,
        mesh=mesh,
        in_specs=(
            P(None, "dp", "tensor"),
            P(None, "dp", "tensor"),
            P(None, "dp", "tensor"),
            P("tensor", None),
            P(None, "dp", "tensor"),
            P(),
            P(),
        ),
        out_specs=(
            P(None, "dp", "tensor"),
            P(None, "dp", "tensor"),
            P(None, "dp", "tensor"),
            P(None, "dp", "tensor"),
            P("dp", "tensor"),
        ),
        check_vma=False,
    )
```

profile of v0, /device:TPU:1, one launch (start us, length us, event | category | flops | bytes accessed | tf_op | source)
XLA Modules:
  0.0 273.3 jit_solution(1171092306402837815)
XLA Ops:
  7.2 1.1 copy.85
  8.3 1.0 copy.86
  9.4 1.3 collective-permute-start.7
  10.7 1.3 collective-permute-start.6
  12.0 10.8 %collective-permute-start.2 = (bf16[2,2,128,256]{2,3,1,0:T(8,128)(2,1)S(1)}, bf16[2,2,128,256]{2,3,1,0:T(8,128)(2,1)S(1)}, u32[]{:S(2)}, u32[]{:S(2)}) collective-permute-start(bf16[2,2,128,256]{2,3,1,0:T(8,128)(2,1)S(1)} %pad_maximum_fusion), channel_id=1, source_target_pairs={{0,16},{8,24},{16,32},{24,40},{32,48},{40,56},{48,64},{56,72},{64,... | collective-permute-start | bytes 786440 | tf_op jit(solution)/shard_map/ppermute | solution.py:18
  22.8 4.3 %collective-permute-start.1 = (bf16[2,2,128,256]{2,3,1,0:T(8,128)(2,1)S(1)}, bf16[2,2,128,256]{2,3,1,0:T(8,128)(2,1)S(1)}, u32[]{:S(2)}, u32[]{:S(2)}) collective-permute-start(bf16[2,2,128,256]{2,3,1,0:T(8,128)(2,1)S(1)} %pad_maximum_fusion), channel_id=1, source_target_pairs={{0,24},{8,32},{16,40},{24,48},{32,56},{40,64},{48,72},{56,80},{64,... | collective-permute-start | bytes 786440 | tf_op jit(solution)/shard_map/ppermute | solution.py:18
  27.1 3.4 %collective-permute-start = (bf16[2,2,128,256]{2,3,1,0:T(8,128)(2,1)S(1)}, bf16[2,2,128,256]{2,3,1,0:T(8,128)(2,1)S(1)}, u32[]{:S(2)}, u32[]{:S(2)}) collective-permute-start(bf16[2,2,128,256]{2,3,1,0:T(8,128)(2,1)S(1)} %pad_maximum_fusion), channel_id=1, source_target_pairs={{0,32},{8,40},{16,48},{24,56},{32,64},{40,72},{48,80},{56,88},{64,... | collective-permute-start | bytes 786440 | tf_op jit(solution)/shard_map/ppermute | solution.py:18
  30.6 0.9 dynamic-slice_reduce_fusion
  31.5 0.1 iota_compare_fusion
  31.5 0.8 pad_dynamic-slice_fusion
  32.3 0.1 copy.87
  32.4 0.1 and_reduce_fusion
  32.5 0.1 broadcast_bitcast_fusion
  32.6 9.1 %collective-permute-done = bf16[2,2,128,256]{2,3,1,0:T(8,128)(2,1)S(1)} collective-permute-done((bf16[2,2,128,256]{2,3,1,0:T(8,128)(2,1)S(1)}, bf16[2,2,128,256]{2,3,1,0:T(8,128)(2,1)S(1)}, u32[]{:S(2)}, u32[]{:S(2)}) %collective-permute-start) | collective-permute-done | bytes 262176 | tf_op jit(solution)/shard_map/ppermute | solution.py:18
  41.7 1.9 collective-permute-start.3
  43.6 1.3 collective-permute-start.5
  44.9 0.1 constant_dynamic-update-slice_fusion.7
  45.0 2.4 collective-permute-start.4
  47.5 0.1 constant_dynamic-update-slice_fusion.5
  47.7 9.7 %collective-permute-done.4 = bf16[2,2,128,256]{2,3,1,0:T(8,128)(2,1)S(1)} collective-permute-done((bf16[2,2,128,256]{2,3,1,0:T(8,128)(2,1)S(1)}, bf16[2,2,128,256]{2,3,1,0:T(8,128)(2,1)S(1)}, u32[]{:S(2)}, u32[]{:S(2)}) %collective-permute-start.4) | collective-permute-done | bytes 262176 | tf_op jit(solution)/shard_map/ppermute | solution.py:18
  57.4 0.1 constant_dynamic-update-slice_fusion.2
  57.5 0.1 constant_dynamic-update-slice_fusion.1
  57.7 0.2 fusion.34
  57.9 0.7 copy-done.8
  58.6 0.9 select_reduce_fusion.1
  59.5 0.5 select_reduce_fusion
  60.0 1.0 convolution_convert_fusion.1
  61.1 1.5 convolution_convert_fusion
  62.6 0.2 reduce-scatter.7.cloned.1.call-start
  62.8 0.8 copy.110
  63.6 7.5 %all-gather.2.cloned.1.call-done = bf16[2,128,2048]{2,1,0:T(8,128)(2,1)} async-done(((bf16[2,128,256]{2,1,0:T(8,128)(2,1)}), bf16[2,128,2048]{2,1,0:T(8,128)(2,1)}) %all-gather.2.cloned.1.call-update) | async-done | bytes 1048592 | tf_op jit(solution)/shard_map/all_gather | solution.py:87
  71.1 3.1 %convolution_bitcast_fusion.2 = f32[2048,256]{0,1:T(8,128)} fusion(bf16[256,2048]{1,0:T(8,128)(2,1)} %bitcast.137, bf16[32,8,2,128]{3,2,1,0:T(2,128)(2,1)} %bitcast.145), kind=kOutput, calls=%fused_computation.8 | convolution fusion | flops 268435456 | bytes 3276800 | tf_op jit(solution)/shard_map/dot_general | solution.py:93
  74.2 2.9 %copy.120 = f32[2048,256]{1,0:T(8,128)} copy(f32[2048,256]{0,1:T(8,128)} %convolution_bitcast_fusion.2) | data formatting | bytes 4194304
  77.2 1.7 convolution_convert_fusion.2
  78.9 0.7 reshape_reshape.3
  79.6 1.0 copy.99
  80.6 2.0 convolution_bitcast_fusion
  82.6 5.0 %copy.101 = f32[2,1152,2,128]{3,2,1,0:T(2,128)} copy(f32[2,1152,2,128]{1,3,2,0:T(8,128)} %convolution_bitcast_fusion) | data formatting | bytes 4718592 | tf_op jit(solution)/shard_map/vhqk,vqhd->vkhd/transpose | solution.py:111
  87.5 4.2 %stack.22 = f32[1,2,9,128,256]{4,3,2,1,0:T(8,128)} reshape(f32[2,1152,2,128]{3,2,1,0:T(2,128)} %copy.101) | data formatting | bytes 4718592 | tf_op jit(solution)/shard_map/stack | solution.py:117
  91.7 3.3 %fusion.35 = f32[2,2,128,1152]{2,3,1,0:T(8,128)} fusion(bf16[2,128,2,128]{1,3,2,0:T(8,128)(2,1)S(1)} %copy.99, bf16[2,1152,2,128]{1,3,2,0:T(8,128)(2,1)} %bitcast.134), kind=kOutput, calls=%fused_computation.76 | convolution fusion | flops 150994944 | bytes 3670016 | tf_op jit(solution)/shard_map/vqhd,vkhd->vhqk/dot_general | solution.py:102
  95.0 5.1 %convolution_bitcast_fusion.1 = f32[2,1152,2,128]{3,1,2,0:T(8,128)} fusion(f32[2,2,128,1152]{2,3,1,0:T(8,128)} %fusion.35, f32[2,2,1152,128]{3,2,1,0:T(8,128)S(1)} %get-tuple-element.38, f32[2,2,128]{2,1,0:T(2,128)S(1)} %log_add_fusion, pred[2,1152]{1,0:T(4,128)(4,1)S(1)} %bitcast.151, bf16[2,128,256]{2,1,0:T(8,128)(2,1)} %param.7), kind=kOutput, calls=%fused_computation.6 | convolution fusion | flops 156305024 | bytes 7213312 | tf_op jit(solution)/shard_map/vhqk,vqhd->vkhd/dot_general | solution.py:114
  100.1 7.8 %copy.98 = f32[2,1152,2,128]{3,2,1,0:T(2,128)} copy(f32[2,1152,2,128]{3,1,2,0:T(8,128)} %convolution_bitcast_fusion.1) | data formatting | bytes 4718592 | tf_op jit(solution)/shard_map/vhqk,vqhd->vkhd/transpose | solution.py:114
  107.9 4.2 %stack.21 = f32[1,2,9,128,256]{4,3,2,1,0:T(8,128)} reshape(f32[2,1152,2,128]{3,2,1,0:T(2,128)} %copy.98) | data formatting | bytes 4718592 | tf_op jit(solution)/shard_map/stack | solution.py:117
  112.1 2.0 constant_dynamic-update-slice_fusion.10
  114.1 0.4 copy-done.2
  114.5 0.2 constant_dynamic-update-slice_fusion.9
  114.6 0.3 convert.14
  115.0 1.8 copy-done.1
  116.8 1.1 slice_bitcast_fusion.8
  117.9 1.3 collective-permute-start.8
  119.2 3.1 %collective-permute-start.13 = (bf16[2,2,128,256]{3,2,1,0:T(8,128)(2,1)S(1)}, bf16[2,2,128,256]{3,2,1,0:T(8,128)(2,1)S(1)}, u32[]{:S(2)}, u32[]{:S(2)}) collective-permute-start(bf16[2,2,128,256]{3,2,1,0:T(8,128)(2,1)S(1)} %get-tuple-element.26), channel_id=1, source_target_pairs={{0,16},{8,24},{16,32},{24,40},{32,48},{40,56},{48,64},{56,72},{64,... | collective-permute-start | bytes 786440 | tf_op jit(solution)/shard_map/ppermute | solution.py:18
  122.3 9.3 %collective-permute-start.12 = (bf16[2,2,128,256]{3,2,1,0:T(8,128)(2,1)S(1)}, bf16[2,2,128,256]{3,2,1,0:T(8,128)(2,1)S(1)}, u32[]{:S(2)}, u32[]{:S(2)}) collective-permute-start(bf16[2,2,128,256]{3,2,1,0:T(8,128)(2,1)S(1)} %get-tuple-element.27), channel_id=1, source_target_pairs={{0,8},{8,16},{16,24},{24,32},{32,40},{40,48},{48,56},{56,64},{64,7... | collective-permute-start | bytes 786440 | tf_op jit(solution)/shard_map/ppermute | solution.py:18
  131.6 1.9 collective-permute-start.11
  133.5 1.3 collective-permute-start.10
  134.8 1.3 collective-permute-start.9
  136.2 8.7 %collective-permute-start.15 = (bf16[2,2,128,256]{3,2,1,0:T(8,128)(2,1)}, bf16[2,2,128,256]{3,2,1,0:T(8,128)(2,1)}, u32[]{:S(2)}, u32[]{:S(2)}) collective-permute-start(bf16[2,2,128,256]{3,2,1,0:T(8,128)(2,1)} %get-tuple-element.31), channel_id=1, source_target_pairs={{0,32},{8,40},{16,48},{24,56},{32,64},{40,72},{48,80},{56,88},{64,... | collective-permute-start | bytes 786440 | tf_op jit(solution)/shard_map/ppermute | solution.py:18
  144.9 0.7 copy-done.7
  145.6 6.9 %collective-permute-start.14 = (bf16[2,2,128,256]{3,2,1,0:T(8,128)(2,1)}, bf16[2,2,128,256]{3,2,1,0:T(8,128)(2,1)}, u32[]{:S(2)}, u32[]{:S(2)}) collective-permute-start(bf16[2,2,128,256]{3,2,1,0:T(8,128)(2,1)} %get-tuple-element.32), channel_id=1, source_target_pairs={{0,24},{8,32},{16,40},{24,48},{32,56},{40,64},{48,72},{56,80},{64,... | collective-permute-start | bytes 786440 | tf_op jit(solution)/shard_map/ppermute | solution.py:18
  152.5 4.2 %fusion.9 = bf16[2,2,128,128]{3,2,1,0:T(8,128)(2,1)S(1)} fusion(bf16[2,1152,2,128]{1,3,2,0:T(8,128)(2,1)} %bitcast.136, f32[2,2,128,1152]{2,3,1,0:T(8,128)} %fusion.35, f32[2,2,1152,128]{3,2,1,0:T(8,128)S(1)} %get-tuple-element.38, f32[2,2,128]{2,1,0:T(2,128)S(1)} %log_add_fusion, pred[2,1152]{1,0:T(4,128)(4,1)S(1)} %bitcast.152), kind=kOutput, calls=%fused_computation.20 | convolution fusion | flops 156370560 | bytes 6033664 | tf_op jit(solution)/shard_map/vhqk,vkhd->vqhd/dot_general | solution.py:107
  156.7 0.8 copy.111
  157.5 1.1 collective-permute-done.14
  158.6 2.0 fusion.19
  160.6 0.7 slice_bitcast_fusion.9
  161.3 105.5 %reduce-scatter.7.cloned.1.call-done = f32[32,256]{1,0:T(8,128)} async-done(((f32[2048,256]{1,0:T(8,128)}), f32[32,256]{1,0:T(8,128)}) %reduce-scatter.7.cloned.1.call-update) | async-done | bytes 32784
  (42 shorter events, 0.6 us)
Async XLA Ops:
  7.2 53.9 %copy-start = (bf16[256,2048]{1,0:T(8,128)(2,1)S(1)}, bf16[256,2048]{1,0:T(8,128)(2,1)}, u32[]{:S(2)}) copy-start(bf16[256,2048]{1,0:T(8,128)(2,1)} %param.10) | copy-start | bytes 3145732
  7.2 64.0 %all-gather.2.cloned.1.call-start = ((), (), s32[]{:S(2)}) async-start(), calls=%async_computation.3 | async-start | bytes 1179648 | tf_op jit(solution)/shard_map/all_gather | solution.py:87
  9.4 48.2 %collective-permute-start.7 = (bf16[2,2,128,256]{2,3,1,0:T(8,128)(2,1)S(1)}, bf16[2,2,128,256]{2,3,1,0:T(8,128)(2,1)S(1)}, u32[]{:S(2)}, u32[]{:S(2)}) collective-permute-start(bf16[2,2,128,256]{2,3,1,0:T(8,128)(2,1)S(1)} %pad_maximum_fusion), channel_id=1, source_target_pairs={{32,0},{40,8},{48,16},{56,24},{64,32},{72,40},{80,48},{88,56},{96,... | collective-permute-start | bytes 786440 | tf_op jit(solution)/shard_map/ppermute | solution.py:18
  10.7 46.8 %collective-permute-start.6 = (bf16[2,2,128,256]{2,3,1,0:T(8,128)(2,1)S(1)}, bf16[2,2,128,256]{2,3,1,0:T(8,128)(2,1)S(1)}, u32[]{:S(2)}, u32[]{:S(2)}) collective-permute-start(bf16[2,2,128,256]{2,3,1,0:T(8,128)(2,1)S(1)} %pad_maximum_fusion), channel_id=1, source_target_pairs={{24,0},{32,8},{40,16},{48,24},{56,32},{64,40},{72,48},{80,56},{88,... | collective-permute-start | bytes 786440 | tf_op jit(solution)/shard_map/ppermute | solution.py:18
  12.0 33.0 %collective-permute-start.2 = (bf16[2,2,128,256]{2,3,1,0:T(8,128)(2,1)S(1)}, bf16[2,2,128,256]{2,3,1,0:T(8,128)(2,1)S(1)}, u32[]{:S(2)}, u32[]{:S(2)}) collective-permute-start(bf16[2,2,128,256]{2,3,1,0:T(8,128)(2,1)S(1)} %pad_maximum_fusion), channel_id=1, source_target_pairs={{0,16},{8,24},{16,32},{24,40},{32,48},{40,56},{48,64},{56,72},{64,... | collective-permute-start | bytes 786440 | tf_op jit(solution)/shard_map/ppermute | solution.py:18
  22.8 20.9 %collective-permute-start.1 = (bf16[2,2,128,256]{2,3,1,0:T(8,128)(2,1)S(1)}, bf16[2,2,128,256]{2,3,1,0:T(8,128)(2,1)S(1)}, u32[]{:S(2)}, u32[]{:S(2)}) collective-permute-start(bf16[2,2,128,256]{2,3,1,0:T(8,128)(2,1)S(1)} %pad_maximum_fusion), channel_id=1, source_target_pairs={{0,24},{8,32},{16,40},{24,48},{32,56},{40,64},{48,72},{56,80},{64,... | collective-permute-start | bytes 786440 | tf_op jit(solution)/shard_map/ppermute | solution.py:18
  27.1 14.5 %collective-permute-start = (bf16[2,2,128,256]{2,3,1,0:T(8,128)(2,1)S(1)}, bf16[2,2,128,256]{2,3,1,0:T(8,128)(2,1)S(1)}, u32[]{:S(2)}, u32[]{:S(2)}) collective-permute-start(bf16[2,2,128,256]{2,3,1,0:T(8,128)(2,1)S(1)} %pad_maximum_fusion), channel_id=1, source_target_pairs={{0,32},{8,40},{16,48},{24,56},{32,64},{40,72},{48,80},{56,88},{64,... | collective-permute-start | bytes 786440 | tf_op jit(solution)/shard_map/ppermute | solution.py:18
  30.5 130.8 %reduce-scatter.5.cloned.1.call-start = ((), (), s32[]{:S(2)}) async-start(), calls=%async_computation.2 | async-start | bytes 1179648 | tf_op jit(solution)/shard_map/reduce_scatter | solution.py:84
  41.7 5.9 %collective-permute-start.3 = (bf16[2,2,128,256]{2,3,1,0:T(8,128)(2,1)S(1)}, bf16[2,2,128,256]{2,3,1,0:T(8,128)(2,1)S(1)}, u32[]{:S(2)}, u32[]{:S(2)}) collective-permute-start(bf16[2,2,128,256]{2,3,1,0:T(8,128)(2,1)S(1)} %pad_maximum_fusion), channel_id=1, source_target_pairs={{0,8},{8,16},{16,24},{24,32},{32,40},{40,48},{48,56},{56,64},{64,7... | collective-permute-start | bytes 786440 | tf_op jit(solution)/shard_map/ppermute | solution.py:18
  43.6 13.8 %collective-permute-start.5 = (bf16[2,2,128,256]{2,3,1,0:T(8,128)(2,1)S(1)}, bf16[2,2,128,256]{2,3,1,0:T(8,128)(2,1)S(1)}, u32[]{:S(2)}, u32[]{:S(2)}) collective-permute-start(bf16[2,2,128,256]{2,3,1,0:T(8,128)(2,1)S(1)} %pad_maximum_fusion), channel_id=1, source_target_pairs={{16,0},{24,8},{32,16},{40,24},{48,32},{56,40},{64,48},{72,56},{80,... | collective-permute-start | bytes 786440 | tf_op jit(solution)/shard_map/ppermute | solution.py:18
  45.0 12.3 %collective-permute-start.4 = (bf16[2,2,128,256]{2,3,1,0:T(8,128)(2,1)S(1)}, bf16[2,2,128,256]{2,3,1,0:T(8,128)(2,1)S(1)}, u32[]{:S(2)}, u32[]{:S(2)}) collective-permute-start(bf16[2,2,128,256]{2,3,1,0:T(8,128)(2,1)S(1)} %pad_maximum_fusion), channel_id=1, source_target_pairs={{8,0},{16,8},{24,16},{32,24},{40,32},{48,40},{56,48},{64,56},{72,6... | collective-permute-start | bytes 786440 | tf_op jit(solution)/shard_map/ppermute | solution.py:18
  57.7 0.9 copy-start.8
  57.9 2.1 copy-start.4
  57.9 2.1 copy-start.3
  62.6 204.2 %reduce-scatter.7.cloned.1.call-start = ((), (), s32[]{:S(2)}) async-start(), calls=%async_computation.4 | async-start | bytes 2129920
  112.1 2.4 copy-start.2
  114.6 2.1 copy-start.1
  117.9 16.9 %collective-permute-start.8 = (bf16[2,2,128,256]{3,2,1,0:T(8,128)(2,1)S(1)}, bf16[2,2,128,256]{3,2,1,0:T(8,128)(2,1)S(1)}, u32[]{:S(2)}, u32[]{:S(2)}) collective-permute-start(bf16[2,2,128,256]{3,2,1,0:T(8,128)(2,1)S(1)} %get-tuple-element.25), channel_id=1, source_target_pairs={{32,0},{40,8},{48,16},{56,24},{64,32},{72,40},{80,48},{88,56},{96,... | collective-permute-start | bytes 786440 | tf_op jit(solution)/shard_map/ppermute | solution.py:18
  119.2 17.0 %collective-permute-start.13 = (bf16[2,2,128,256]{3,2,1,0:T(8,128)(2,1)S(1)}, bf16[2,2,128,256]{3,2,1,0:T(8,128)(2,1)S(1)}, u32[]{:S(2)}, u32[]{:S(2)}) collective-permute-start(bf16[2,2,128,256]{3,2,1,0:T(8,128)(2,1)S(1)} %get-tuple-element.26), channel_id=1, source_target_pairs={{0,16},{8,24},{16,32},{24,40},{32,48},{40,56},{48,64},{56,72},{64,... | collective-permute-start | bytes 786440 | tf_op jit(solution)/shard_map/ppermute | solution.py:18
  122.3 22.6 %collective-permute-start.12 = (bf16[2,2,128,256]{3,2,1,0:T(8,128)(2,1)S(1)}, bf16[2,2,128,256]{3,2,1,0:T(8,128)(2,1)S(1)}, u32[]{:S(2)}, u32[]{:S(2)}) collective-permute-start(bf16[2,2,128,256]{3,2,1,0:T(8,128)(2,1)S(1)} %get-tuple-element.27), channel_id=1, source_target_pairs={{0,8},{8,16},{16,24},{24,32},{32,40},{40,48},{48,56},{56,64},{64,7... | collective-permute-start | bytes 786440 | tf_op jit(solution)/shard_map/ppermute | solution.py:18
  131.6 25.9 %collective-permute-start.11 = (bf16[2,2,128,256]{3,2,1,0:T(8,128)(2,1)}, bf16[2,2,128,256]{3,2,1,0:T(8,128)(2,1)}, u32[]{:S(2)}, u32[]{:S(2)}) collective-permute-start(bf16[2,2,128,256]{3,2,1,0:T(8,128)(2,1)} %get-tuple-element.28), channel_id=1, source_target_pairs={{8,0},{16,8},{24,16},{32,24},{40,32},{48,40},{56,48},{64,56},{72,6... | collective-permute-start | bytes 786440 | tf_op jit(solution)/shard_map/ppermute | solution.py:18
  133.5 23.9 %collective-permute-start.10 = (bf16[2,2,128,256]{3,2,1,0:T(8,128)(2,1)}, bf16[2,2,128,256]{3,2,1,0:T(8,128)(2,1)}, u32[]{:S(2)}, u32[]{:S(2)}) collective-permute-start(bf16[2,2,128,256]{3,2,1,0:T(8,128)(2,1)} %get-tuple-element.29), channel_id=1, source_target_pairs={{16,0},{24,8},{32,16},{40,24},{48,32},{56,40},{64,48},{72,56},{80,... | collective-permute-start | bytes 786440 | tf_op jit(solution)/shard_map/ppermute | solution.py:18
  134.8 10.0 %copy-start.5 = (bf16[2,2,128,256]{3,2,1,0:T(8,128)(2,1)}, bf16[2,2,128,256]{3,2,1,0:T(8,128)(2,1)S(1)}, u32[]{:S(2)}) copy-start(bf16[2,2,128,256]{3,2,1,0:T(8,128)(2,1)S(1)} %collective-permute-done.8) | copy-start | bytes 786436
  134.8 22.6 %collective-permute-start.9 = (bf16[2,2,128,256]{3,2,1,0:T(8,128)(2,1)}, bf16[2,2,128,256]{3,2,1,0:T(8,128)(2,1)}, u32[]{:S(2)}, u32[]{:S(2)}) collective-permute-start(bf16[2,2,128,256]{3,2,1,0:T(8,128)(2,1)} %get-tuple-element.30), channel_id=1, source_target_pairs={{24,0},{32,8},{40,16},{48,24},{56,32},{64,40},{72,48},{80,56},{88,... | collective-permute-start | bytes 786440 | tf_op jit(solution)/shard_map/ppermute | solution.py:18
  136.1 8.7 %copy-start.6 = (bf16[2,2,128,256]{3,2,1,0:T(8,128)(2,1)}, bf16[2,2,128,256]{3,2,1,0:T(8,128)(2,1)S(1)}, u32[]{:S(2)}) copy-start(bf16[2,2,128,256]{3,2,1,0:T(8,128)(2,1)S(1)} %collective-permute-done.13) | copy-start | bytes 786436
  136.2 21.3 %collective-permute-start.15 = (bf16[2,2,128,256]{3,2,1,0:T(8,128)(2,1)}, bf16[2,2,128,256]{3,2,1,0:T(8,128)(2,1)}, u32[]{:S(2)}, u32[]{:S(2)}) collective-permute-start(bf16[2,2,128,256]{3,2,1,0:T(8,128)(2,1)} %get-tuple-element.31), channel_id=1, source_target_pairs={{0,32},{8,40},{16,48},{24,56},{32,64},{40,72},{48,80},{56,88},{64,... | collective-permute-start | bytes 786440 | tf_op jit(solution)/shard_map/ppermute | solution.py:18
  144.9 0.7 copy-start.7
  145.6 13.0 %collective-permute-start.14 = (bf16[2,2,128,256]{3,2,1,0:T(8,128)(2,1)}, bf16[2,2,128,256]{3,2,1,0:T(8,128)(2,1)}, u32[]{:S(2)}, u32[]{:S(2)}) collective-permute-start(bf16[2,2,128,256]{3,2,1,0:T(8,128)(2,1)} %get-tuple-element.32), channel_id=1, source_target_pairs={{0,24},{8,32},{16,40},{24,48},{32,56},{40,64},{48,72},{56,80},{64,... | collective-permute-start | bytes 786440 | tf_op jit(solution)/shard_map/ppermute | solution.py:18
Sparse Core Ops, SparseCore 0:
  30.6 40.4 all-gather.1
  74.5 40.4 reduce-scatter.4
  120.3 146.4 reduce-scatter.6
where the time goes:
time: 278 us; the launch traced here: 273 us
  waiting for transfers between devices  133 us (48%)
  starting transfers between devices  60.7 us (22%)
  local copies, waits for them, and re-layouts  39.5 us (14%)
  matrix products  22.8 us (8%)
  between operations  14.2 us (5%)
  other arithmetic  3.09 us (1%)
    unnamed x4, waiting for transfers between devices  106 us
    ppermute x16, starting transfers between devices, from_behind(): return lax.ppermute(block, axis, route)  60.4 us
    ppermute x16, waiting for transfers between devices, from_behind(): return lax.ppermute(block, axis, route)  19.9 us
    unnamed x32, local copies, waits for them, and re-layouts  11.9 us
    another operation x3, local copies, waits for them, and re-layouts, local(): jnp.stack([key_terms, value_terms])  8.48 us
    transpose x1, local copies, waits for them, and re-layouts, local(): jnp.einsum('vhqk,vqhd->vkhd', score_grads, query_heads, preferred_element...  7.78 us
    all_gather x1, waiting for transfers between devices, local(): grad_full = lax.all_gather(out_grad, 'tensor', axis=2, tiled=True)  7.55 us
  transfers between devices with their start and end apart: 19, of which 5 were waited for; matrix products, arithmetic and copies ran while one was open for 22% of the time, Pallas kernels for 0%

commit v1 on v0

v1 whole, which is shorter than its diff:
```python
import functools
import math

import jax
import jax.numpy as jnp
from jax import lax
from jax.experimental import pallas as pl
from jax.experimental.pallas import tpu as pltpu
from jax.sharding import PartitionSpec as P

HD = 128
REACH = 4
NEGATIVE = -1e30
RING = 8
ROW = 4
MESH = pl.DeviceIdType.MESH
VMEM = pltpu.VMEM
F32 = jnp.float32
BF16 = jnp.bfloat16

OFFSETS = tuple(o for o in range(-REACH, REACH + 1) if o != 0)
FAR_FIRST = tuple(sorted(OFFSETS, key=lambda o: -abs(o)))


def slot_of(offset):
    return offset + REACH if offset < 0 else offset + REACH - 1


def wrap(index, size):
    return lax.rem(index + size, size)


def dot_nn(a, b):
    return lax.dot_general(a, b, (((1,), (0,)), ((), ())), preferred_element_type=F32)


def dot_nt(a, b):
    return lax.dot_general(a, b, (((1,), (1,)), ((), ())), preferred_element_type=F32)


def dot_tn(a, b):
    return lax.dot_general(a, b, (((0,), (0,)), ((), ())), preferred_element_type=F32)


def lists_block(lists_ref, counts_ref, variant, row, block):
    count = counts_ref[variant, row]
    hit = jnp.int32(0)
    for slot in range(lists_ref.shape[2]):
        same = (lists_ref[variant, row, slot] == block) & (count > slot)
        hit = jnp.where(same, 1, hit)
    return hit


def greet(partners):
    barrier = pltpu.get_barrier_semaphore()
    for partner in partners:
        pl.semaphore_signal(barrier, inc=1, device_id=partner, device_id_type=MESH)
    pl.semaphore_wait(barrier, len(partners))


def fetch_kernel(
    lists_ref, counts_ref, k_ref, v_ref, og_ref, win_ref, full_ref,
    picked, kv_send, kv_recv, ring_send, ring_recv, own_sem,
):
    d = lax.axis_index("dp")
    t = lax.axis_index("tensor")
    n_dp = lax.axis_size("dp")
    sides = ((0, -1), (1, 1))
    near = [(wrap(d + o, n_dp), t) for o in OFFSETS]
    beside = [(d, wrap(t + step, RING)) for _, step in sides]
    own = pltpu.make_async_copy(og_ref, full_ref.at[t], own_sem)
    own.start()
    greet(near + beside)

    def hop(side, step, distance, half):
        source = wrap(t - step * (distance - 1), RING)
        origin = og_ref.at[half] if distance == 1 else full_ref.at[source, half]
        return pltpu.make_async_remote_copy(
            src_ref=origin,
            dst_ref=full_ref.at[source, half],
            send_sem=ring_send.at[side, distance - 1, half],
            recv_sem=ring_recv.at[side, distance - 1, half],
            device_id=(d, wrap(t + step, RING)),
            device_id_type=MESH,
        )

    hops = {}
    for half in range(2):
        for side, step in sides:
            hops[side, 1, half] = hop(side, step, 1, half)
            hops[side, 1, half].start()

    sends = []
    for o in FAR_FIRST:
        e = wrap(d + o, n_dp)
        slot = slot_of(o)
        second = lists_block(lists_ref, counts_ref, 1, e, d) == 1
        picked[slot, 0] = jnp.where(second, k_ref[1], k_ref[0])
        picked[slot, 1] = jnp.where(second, v_ref[1], v_ref[0])
        copy = pltpu.make_async_remote_copy(
            src_ref=picked.at[slot],
            dst_ref=win_ref.at[slot_of(-o)],
            send_sem=kv_send.at[slot],
            recv_sem=kv_recv.at[slot_of(-o)],
            device_id=(e, t),
            device_id_type=MESH,
        )
        copy.start()
        sends.append(copy)

    for distance in range(1, 4):
        for half in range(2):
            for side, step in sides:
                hops[side, distance, half].wait_recv()
                if distance < 3 or half == side:
                    hops[side, distance + 1, half] = hop(side, step, distance + 1, half)
                    hops[side, distance + 1, half].start()
    for side in range(2):
        hops[side, 4, side].wait_recv()
    for copy in hops.values():
        copy.wait_send()
    for copy in sends:
        copy.wait()
    own.wait()


def attend_kernel(
    lists_ref, counts_ref, q_ref, k_ref, v_ref, w_ref, win_ref, full_ref,
    dq_ref, own_ref, term_ref, part_ref, proj_ref,
    grad, scores, prob_grads, attended,
):
    d = lax.axis_index("dp")
    scale = 1.0 / math.sqrt(HD)
    width = q_ref.shape[2]
    heads = width // HD
    variants = q_ref.shape[0]
    rows = q_ref.shape[1]

    total = jnp.zeros((variants * rows, width), F32)
    for z in range(RING):
        block = full_ref[z].reshape(variants * rows, width)
        total = total + dot_nt(block, w_ref[:, z * width:(z + 1) * width])
    grad[...] = total.astype(BF16).reshape(variants, rows, width)

    pairs = [(None, v) for v in range(variants)]
    for o in OFFSETS:
        first = lists_block(lists_ref, counts_ref, 0, d, d + o)
        second = lists_block(lists_ref, counts_ref, 1, d, d + o)
        pairs.append((o, (second, (first + second) > 0)))

    def cols(h):
        return slice(h * HD, (h + 1) * HD)

    def key_of(pair, h):
        o, which = pair
        return k_ref[which, :, cols(h)] if o is None else win_ref[slot_of(o), 0, :, cols(h)]

    def value_of(pair, h):
        o, which = pair
        return v_ref[which, :, cols(h)] if o is None else win_ref[slot_of(o), 1, :, cols(h)]

    def of_variant(pair, ref, h):
        o, which = pair
        return ref[which if o is None else which[0], :, cols(h)]

    def pick(pair, stats):
        o, which = pair
        return stats[which] if o is None else jnp.where(which[0] == 1, stats[1], stats[0])

    def merge(pair, stats, new, combine, neutral):
        o, which = pair
        if o is None:
            stats[which] = combine(stats[which], new)
        else:
            for v in range(variants):
                stats[v] = combine(stats[v], jnp.where(which[0] == v, new, neutral))

    for h in range(heads):
        tops = [jnp.full((1, rows), NEGATIVE, F32) for _ in range(variants)]
        for p, pair in enumerate(pairs):
            s = dot_nt(key_of(pair, h), of_variant(pair, q_ref, h)) * scale
            if pair[0] is not None:
                s = jnp.where(pair[1][1], s, NEGATIVE)
            scores[p, h] = s
            merge(pair, tops, jnp.max(s, axis=0, keepdims=True), jnp.maximum, NEGATIVE)
            prob_grads[p, h] = dot_nt(value_of(pair, h), of_variant(pair, grad, h))
        sums = [jnp.zeros((1, rows), F32) for _ in range(variants)]
        for p, pair in enumerate(pairs):
            e = jnp.exp(scores[p, h] - pick(pair, tops))
            scores[p, h] = e
            merge(pair, sums, jnp.sum(e, axis=0, keepdims=True), jnp.add, 0.0)
        inverse = [1.0 / s for s in sums]
        deltas = [jnp.zeros((1, rows), F32) for _ in range(variants)]
        outs = [jnp.zeros((rows, HD), F32) for _ in range(variants)]
        for p, pair in enumerate(pairs):
            prob = scores[p, h] * pick(pair, inverse)
            scores[p, h] = prob
            low = prob.astype(BF16)
            merge(pair, deltas, jnp.sum(prob * prob_grads[p, h], axis=0, keepdims=True), jnp.add, 0.0)
            merge(pair, outs, dot_tn(low, value_of(pair, h)), jnp.add, 0.0)
            term = dot_nn(low, of_variant(pair, grad, h))
            if pair[0] is None:
                own_ref[1, pair[1], :, cols(h)] = term
            else:
                term_ref[slot_of(pair[0]), 1, :, cols(h)] = term.astype(BF16)
        for v in range(variants):
            attended[v, :, cols(h)] = outs[v].astype(BF16)
        dqs = [jnp.zeros((rows, HD), F32) for _ in range(variants)]
        for p, pair in enumerate(pairs):
            ds = (scores[p, h] * (prob_grads[p, h] - pick(pair, deltas)) * scale).astype(BF16)
            merge(pair, dqs, dot_tn(ds, key_of(pair, h)), jnp.add, 0.0)
            term = dot_nn(ds, of_variant(pair, q_ref, h))
            if pair[0] is None:
                own_ref[0, pair[1], :, cols(h)] = term
            else:
                term_ref[slot_of(pair[0]), 0, :, cols(h)] = term.astype(BF16)
        for v in range(variants):
            dq_ref[v, :, cols(h)] = dqs[v].astype(BF16)

    flat = attended[...].reshape(variants * rows, width)
    share = width // RING
    for z in range(RING):
        part = dot_nn(flat, w_ref[:, z * width:(z + 1) * width])
        part_ref[z] = part.astype(BF16).reshape(variants, rows, width)
        block = full_ref[z].reshape(variants * rows, width)
        low = dot_tn(block, flat).astype(BF16)
        for b in range(RING):
            proj_ref[b % 2, z, pl.ds((b // 2) * share, share)] = low[b * share:(b + 1) * share]


def ring_reduce(own, landed, send_sem, recv_sem, me, device_at):
    sides = ((0, -1), (1, 1))
    copies = {}

    def send(side, half, distance):
        step = sides[side][1]
        first = distance == (4 if side == half else 3)
        target = wrap(me + step * distance, RING)
        origin = own.at[target, half] if first else landed.at[side, half, distance]
        copy = pltpu.make_async_remote_copy(
            src_ref=origin,
            dst_ref=landed.at[side, half, distance - 1],
            send_sem=send_sem.at[side, half, distance - 1],
            recv_sem=recv_sem.at[side, half, distance - 1],
            device_id=device_at(wrap(me + step, RING)),
            device_id_type=MESH,
        )
        copy.start()
        copies[side, half, distance] = copy

    def begin():
        for half in range(2):
            for side in range(2):
                start = half if side == 0 else 1 - half
                send(side, start, 4 if side == start else 3)

    def advance(distance, side, half):
        if (side, half, distance) not in copies:
            return
        copies[side, half, distance].wait_recv()
        if distance > 1:
            target = wrap(me + sides[side][1] * (distance - 1), RING)
            here = landed.at[side, half, distance - 1]
            here[...] = (here[...].astype(F32) + own[target, half].astype(F32)).astype(BF16)
            send(side, half, distance - 1)

    def result(half):
        return (
            own[me, half].astype(F32)
            + landed[0, half, 0].astype(F32)
            + landed[1, half, 0].astype(F32)
        )

    def finish():
        for copy in copies.values():
            copy.wait_send()

    return begin, advance, result, finish


CORE_ORDER = (4, 3, -3, 2, -2, 1, -1, 0)


def return_kernel(
    term_ref, part_ref, proj_ref, back_ref, layer_ref, grad_ref,
    layer_land, paired, pair_land, proj_land, row_send_buf, row_land,
    term_send, term_recv, layer_send, layer_recv, pair_send, pair_recv,
    proj_send, proj_recv, row_send, row_recv,
):
    d = lax.axis_index("dp")
    t = lax.axis_index("tensor")
    n_dp = lax.axis_size("dp")
    core = lax.rem(d, 2)
    x = lax.rem(d // 2, ROW)
    y = d // (2 * ROW)

    def at(yy, xx, cc):
        return ((yy * ROW + xx) * 2 + cc, t)

    near = [(wrap(d + o, n_dp), t) for o in OFFSETS]
    beside = [(d, wrap(t + s, RING)) for s in (-1, 1)]
    above = [at(wrap(y + s, RING), x, core) for s in (-1, 1)]
    row = [at(y, lax.rem(x + s, ROW), core) for s in range(1, ROW)]
    greet(near + beside + above + row)

    layer_begin, layer_advance, layer_result, layer_finish = ring_reduce(
        part_ref, layer_land, layer_send, layer_recv, t, lambda z: (d, z)
    )
    layer_begin()

    swaps = []
    for j, r in enumerate(CORE_ORDER):
        chunk = wrap(y + r, RING)
        copy = pltpu.make_async_remote_copy(
            src_ref=proj_ref.at[1 - core, chunk],
            dst_ref=pair_land.at[chunk],
            send_sem=pair_send.at[j],
            recv_sem=pair_recv.at[j],
            device_id=at(y, x, 1 - core),
            device_id_type=MESH,
        )
        copy.start()
        swaps.append(copy)

    terms = []
    for o in FAR_FIRST:
        copy = pltpu.make_async_remote_copy(
            src_ref=term_ref.at[slot_of(o)],
            dst_ref=back_ref.at[slot_of(-o)],
            send_sem=term_send.at[slot_of(o)],
            recv_sem=term_recv.at[slot_of(-o)],
            device_id=(wrap(d + o, n_dp), t),
            device_id_type=MESH,
        )
        copy.start()
        terms.append(copy)

    half_rows = paired.shape[2]
    for j, r in enumerate(CORE_ORDER):
        chunk = wrap(y + r, RING)
        swaps[j].wait_recv()
        for half in range(2):
            span = pl.ds(half * half_rows, half_rows)
            both = proj_ref[core, chunk, span].astype(F32) + pair_land[chunk, span].astype(F32)
            paired[chunk, half] = both.astype(BF16)

    proj_begin, proj_advance, proj_result, proj_finish = ring_reduce(
        paired, proj_land, proj_send, proj_recv, y, lambda yy: at(yy, x, core)
    )
    proj_begin()

    for distance in (4, 3, 2, 1):
        for half in range(2):
            for side in range(2):
                layer_advance(distance, side, half)
                proj_advance(distance, side, half)

    share = row_land.shape[1]
    for half in range(2):
        piece = proj_result(half).astype(BF16)
        for part in range(half_rows // share):
            row_send_buf[half * (half_rows // share) + part] = piece[part * share:(part + 1) * share]
    rows = []
    for s in range(1, ROW):
        xx = lax.rem(x + s, ROW)
        copy = pltpu.make_async_remote_copy(
            src_ref=row_send_buf.at[xx],
            dst_ref=row_land.at[s - 1],
            send_sem=row_send.at[s - 1],
            recv_sem=row_recv.at[s - 1],
            device_id=at(y, xx, core),
            device_id_type=MESH,
        )
        copy.start()
        rows.append(copy)
    for half in range(2):
        layer_ref[half] = layer_result(half).astype(BF16)
    total = row_send_buf[x].astype(F32)
    for s in range(ROW - 1):
        rows[s].wait_recv()
        total = total + row_land[s].astype(F32)
    grad_ref[...] = total
    for copy in rows:
        copy.wait_send()
    for copy in swaps:
        copy.wait_send()
    layer_finish()
    proj_finish()
    for copy in terms:
        copy.wait()


def settle_kernel(
    lists_ref, counts_ref, own_ref, back_ref, layer_in, grad_in, layer_ref, dk_ref, dv_ref, grad_ref
):
    d = lax.axis_index("dp")
    n_dp = lax.axis_size("dp")
    layer_ref[...] = layer_in[...]
    grad_ref[...] = grad_in[...]
    second = [
        lists_block(lists_ref, counts_ref, 1, wrap(d + o, n_dp), d) == 1 for o in OFFSETS
    ]
    for which, out in enumerate((dk_ref, dv_ref)):
        first_sum = own_ref[which, 0]
        second_sum = own_ref[which, 1]
        for o, pick in zip(OFFSETS, second):
            term = back_ref[slot_of(o), which].astype(F32)
            first_sum = first_sum + jnp.where(pick, 0.0, term)
            second_sum = second_sum + jnp.where(pick, term, 0.0)
        out[0] = first_sum.astype(BF16)
        out[1] = second_sum.astype(BF16)


def local(queries, key_rows, value_rows, out_weight, out_grad, ibd_lists, ibd_counts):
    variants, rows, width = queries.shape
    n = len(OFFSETS)
    smem = pl.BlockSpec(memory_space=pltpu.SMEM)
    vmem = pl.BlockSpec(memory_space=VMEM)
    anywhere = pl.BlockSpec(memory_space=pl.ANY)
    dma = pltpu.SemaphoreType.DMA
    shape = jax.ShapeDtypeStruct
    limit = 48 * 1024 * 1024
    share = width // RING

    window, full = pl.pallas_call(
        fetch_kernel,
        out_shape=(
            shape((n, 2, rows, width), BF16),
            shape((RING, variants, rows, width), BF16),
        ),
        in_specs=[smem, smem, vmem, vmem, anywhere],
        out_specs=(anywhere, anywhere),
        scratch_shapes=[
            VMEM((n, 2, rows, width), BF16),
            dma((n,)), dma((n,)), dma((2, 4, 2)), dma((2, 4, 2)), dma,
        ],
        compiler_params=pltpu.CompilerParams(
            collective_id=0, has_side_effects=True, vmem_limit_bytes=limit
        ),
        name="fetch",
    )(ibd_lists, ibd_counts, key_rows, value_rows, out_grad)

    dq, own, term, part, proj = pl.pallas_call(
        attend_kernel,
        out_shape=(
            shape((variants, rows, width), BF16),
            shape((2, variants, rows, width), F32),
            shape((n, 2, rows, width), BF16),
            shape((RING, variants, rows, width), BF16),
            shape((2, RING, ROW * share, width), BF16),
        ),
        in_specs=[smem, smem] + [vmem] * 6,
        out_specs=(vmem,) * 5,
        scratch_shapes=[
            VMEM((variants, rows, width), BF16),
            VMEM((n + variants, width // HD, rows, rows), F32),
            VMEM((n + variants, width // HD, rows, rows), F32),
            VMEM((variants, rows, width), BF16),
        ],
        compiler_params=pltpu.CompilerParams(vmem_limit_bytes=limit),
        name="attend",
    )(ibd_lists, ibd_counts, queries, key_rows, value_rows, out_weight, window, full)

    half_rows = ROW * share // 2
    back, layer, proj_sum = pl.pallas_call(
        return_kernel,
        out_shape=(
            shape((n, 2, rows, width), BF16),
            shape((variants, rows, width), BF16),
            shape((share, width), F32),
        ),
        in_specs=[anywhere, vmem, vmem],
        out_specs=(anywhere, vmem, vmem),
        scratch_shapes=[
            VMEM((2, 2, 4, rows, width), BF16),
            VMEM((RING, 2, half_rows, width), BF16),
            VMEM((RING, ROW * share, width), BF16),
            VMEM((2, 2, 4, half_rows, width), BF16),
            VMEM((ROW, share, width), BF16),
            VMEM((ROW - 1, share, width), BF16),
            dma((n,)), dma((n,)), dma((2, 2, 4)), dma((2, 2, 4)),
            dma((len(CORE_ORDER),)), dma((len(CORE_ORDER),)),
            dma((2, 2, 4)), dma((2, 2, 4)), dma((ROW - 1,)), dma((ROW - 1,)),
        ],
        compiler_params=pltpu.CompilerParams(
            collective_id=1, has_side_effects=True, vmem_limit_bytes=limit
        ),
        name="return",
    )(term, part, proj)

    layer_out, key_grad, value_grad, proj_grad = pl.pallas_call(
        settle_kernel,
        out_shape=(
            shape((variants, rows, width), BF16),
            shape((variants, rows, width), BF16),
            shape((variants, rows, width), BF16),
            shape((share, width), F32),
        ),
        in_specs=[smem, smem] + [vmem] * 4,
        out_specs=(vmem,) * 4,
        compiler_params=pltpu.CompilerParams(vmem_limit_bytes=limit),
        name="settle",
    )(ibd_lists, ibd_counts, own, back, layer, proj_sum)
    return (layer_out, dq, key_grad, value_grad, proj_grad)


def solution(mesh):
    spec = P(None, "dp", "tensor")
    return jax.shard_map(
        local,
        mesh=mesh,
        in_specs=(spec, spec, spec, P("tensor", None), spec, P(), P()),
        out_specs=(spec, spec, spec, spec, P("dp", "tensor")),
        check_vma=False,
    )
```

time: 278 us -> 82.3 us (0.30); the launches traced: 273 us -> 82 us
  waiting for transfers between devices: 133 us -> 0 us
  Pallas kernels: 0 us -> 74.6 us
  starting transfers between devices: 60.7 us -> 0 us
  local copies, waits for them, and re-layouts: 39.5 us -> 6.7 us
  matrix products: 22.8 us -> 0 us
  between operations: 14.2 us -> 0.68 us
  other arithmetic: 3.09 us -> 0 us
    unnamed x4 -> x0, waiting for transfers between devices: 106 us -> none
    pallas_call x0 -> x4, Pallas kernels: none -> 74.6 us  [the longest x1 34.5 us: local(): pl.pallas_call(return_kernel, out_shape=(shape((n, 2, rows, width), BF16)...]
    ppermute x16 -> x0, starting transfers between devices: 60.4 us -> none  [from_behind(): return lax.ppermute(block, axis, route)]
    dot_general x9 -> x0, matrix products: 22.8 us -> none  [the longest x1 5.12 us: local(): jnp.einsum('vhqk,vqhd->vkhd', score_grads, query_heads, preferred_element...]
    ppermute x16 -> x0, waiting for transfers between devices: 19.9 us -> none  [from_behind(): return lax.ppermute(block, axis, route)]
    transpose x2 -> x0, local copies, waits for them, and re-layouts: 12.7 us -> none  [the longest x1 7.78 us: local(): jnp.einsum('vhqk,vqhd->vkhd', score_grads, query_heads, preferred_element...]
    another operation x5 -> x0, local copies, waits for them, and re-layouts: 10.2 us -> none  [the longest x3 8.48 us: local(): jnp.stack([key_terms, value_terms])]
    all_gather x1 -> x0, waiting for transfers between devices: 7.55 us -> none  [local(): grad_full = lax.all_gather(out_grad, 'tensor', axis=2, tiled=True)]
  transfers between devices with their start and end apart: 19 -> 0, of which waited for: 5 -> 0; matrix products, arithmetic and copies ran while one was open for 22% -> 0% of each run, Pallas kernels for 0% -> 0%
where the time goes in v1:
time: 82.3 us; the launch traced here: 82 us
  Pallas kernels  74.6 us (91%)
  local copies, waits for them, and re-layouts  6.7 us (8%)
    pallas_call x1, Pallas kernels, local(): pl.pallas_call(return_kernel, out_shape=(shape((n, 2, rows, width), BF16)...  34.5 us
    pallas_call x1, Pallas kernels, local(): pl.pallas_call(fetch_kernel, out_shape=(shape((n, 2, rows, width), BF16),...  31.3 us
    unnamed x17, local copies, waits for them, and re-layouts  6.7 us
    pallas_call x1, Pallas kernels, local(): pl.pallas_call(attend_kernel, out_shape=(shape((variants, rows, width), B...  5.94 us
    pallas_call x1, Pallas kernels, local(): pl.pallas_call(settle_kernel, out_shape=(shape((variants, rows, width), B...  2.87 us

profile of v1, /device:TPU:1, one launch (start us, length us, event | category | flops | bytes accessed | tf_op | source)
XLA Modules:
  0.0 82.0 jit_solution(8457469343988062510)
XLA Ops:
  0.6 0.0 copy-start.7
  0.6 0.8 copy.14.lists_ref
  1.4 0.0 copy-done.7
  1.4 0.0 copy-start.3
  1.5 0.9 %copy-done.3 = bf16[2,128,256]{2,1,0:T(8,128)(2,1)S(1)} copy-done((bf16[2,128,256]{2,1,0:T(8,128)(2,1)S(1)}, bf16[2,128,256]{2,1,0:T(8,128)(2,1)}, u32[]{:S(2)}) %copy-start.3) | copy-done | bytes 131096
  2.4 0.0 copy-start.4
  2.4 0.9 %copy-done.4 = bf16[2,128,256]{2,1,0:T(8,128)(2,1)S(1)} copy-done((bf16[2,128,256]{2,1,0:T(8,128)(2,1)S(1)}, bf16[2,128,256]{2,1,0:T(8,128)(2,1)}, u32[]{:S(2)}) %copy-start.4) | copy-done | bytes 131096
  3.3 0.0 copy-start.5
  3.3 0.9 %copy-done.5 = bf16[2,128,256]{2,1,0:T(8,128)(2,1)S(1)} copy-done((bf16[2,128,256]{2,1,0:T(8,128)(2,1)S(1)}, bf16[2,128,256]{2,1,0:T(8,128)(2,1)}, u32[]{:S(2)}) %copy-start.5) | copy-done | bytes 131096
  4.2 0.0 copy-start.6
  4.2 31.3 %fetch.1 = (bf16[8,2,128,256]{3,2,1,0:T(8,128)(2,1)S(1)}, bf16[8,2,128,256]{3,2,1,0:T(8,128)(2,1)S(1)}) custom-call(s32[2,64,9]{2,1,0:T(8,128)S(1)} %copy.14.lists_ref, s32[2,64]{1,0:T(2,128)S(1)} %copy-done.7, bf16[2,128,256]{2,1,0:T(8,128)(2,1)S(1)} %copy-done.3, bf16[2,128,256]{2,1,0:T(8,128)(2,1)S(1)} %copy-done.4, bf16[2,128,256]{2,1,0:T(8,128)(2,1)S(1)} %copy-done.5), custom_call_target="tpu_custom_call" | custom-call | tf_op jit(solution)/shard_map/fetch/pallas_call | solution.py:425
  35.5 0.0 copy-start.1
  35.5 1.0 %copy-done.1 = bf16[8,2,128,256]{3,2,1,0:T(8,128)(2,1)} copy-done((bf16[8,2,128,256]{3,2,1,0:T(8,128)(2,1)}, bf16[8,2,128,256]{3,2,1,0:T(8,128)(2,1)S(1)}, u32[]{:S(2)}) %copy-start.1) | copy-done | bytes 1048600
  36.5 0.0 copy-start.2
  36.5 1.0 %copy-done.2 = bf16[8,2,128,256]{3,2,1,0:T(8,128)(2,1)} copy-done((bf16[8,2,128,256]{3,2,1,0:T(8,128)(2,1)}, bf16[8,2,128,256]{3,2,1,0:T(8,128)(2,1)S(1)}, u32[]{:S(2)}) %copy-start.2) | copy-done | bytes 1048600
  37.5 0.0 copy-done.6
  37.5 0.0 copy-start
  37.5 1.2 %copy-done = bf16[256,2048]{1,0:T(8,128)(2,1)S(1)} copy-done((bf16[256,2048]{1,0:T(8,128)(2,1)S(1)}, bf16[256,2048]{1,0:T(8,128)(2,1)}, u32[]{:S(2)}) %copy-start) | copy-done | bytes 1048600
  38.7 5.9 %attend.1 = (bf16[2,128,256]{2,1,0:T(8,128)(2,1)}, f32[2,2,128,256]{3,2,1,0:T(8,128)S(1)}, bf16[8,2,128,256]{3,2,1,0:T(8,128)(2,1)S(1)}, bf16[8,2,128,256]{3,2,1...) custom-call(s32[2,64,9]{2,1,0:T(8,128)S(1)} %copy.14.lists_ref, s32[2,64]{1,0:T(2,128)S(1)} %copy-done.7, ...), custom_call_target="tpu_custom_call" | custom-call | tf_op jit(solution)/shard_map/attend/pallas_call | solution.py:443
  44.6 34.5 %return.1 = (bf16[8,2,128,256]{3,2,1,0:T(8,128)(2,1)S(1)}, bf16[2,128,256]{2,1,0:T(8,128)(2,1)S(1)}, f32[32,256]{1,0:T(8,128)S(1)}) custom-call(bf16[8,2,128,256]{3,2,1,0:T(8,128)(2,1)S(1)} %get-tuple-element.22.term_ref, bf16[8,2,128,256]{3,2,1,0:T(8,128)(2,1)S(1)} %get-tuple-element.23.part_ref, bf16[2,8,128,256]{3,2,1,0:T(8,128)(2,1)S(1)} %get-tuple-element.24.proj_ref), custom_call_target="tpu_custom_call" | custom-call | tf_op jit(solution)/shard_map/return/pallas_call | solution.py:465
  79.1 2.9 %settle.1 = (bf16[2,128,256]{2,1,0:T(8,128)(2,1)}, bf16[2,128,256]{2,1,0:T(8,128)(2,1)}, bf16[2,128,256]{2,1,0:T(8,128)(2,1)}, f32[32,256]{1,0:T(8,128)}) custom-call(s32[2,64,9]{2,1,0:T(8,128)S(1)} %copy.14.lists_ref, s32[2,64]{1,0:T(2,128)S(1)} %copy-done.7, f32[2,2,128,256]{3,2,1,0:T(8,128)S(1)} %get-tuple-element.21.own_ref, ...), custom_call_target="tpu_custom_call" | custom-call | tf_op jit(solution)/shard_map/settle/pallas_call | solution.py:491
Async XLA Ops:
  0.6 0.8 copy-start.7
  1.4 0.9 %copy-start.3 = (bf16[2,128,256]{2,1,0:T(8,128)(2,1)S(1)}, bf16[2,128,256]{2,1,0:T(8,128)(2,1)}, u32[]{:S(2)}) copy-start(bf16[2,128,256]{2,1,0:T(8,128)(2,1)} %k_ref.3) | copy-start | bytes 393220
  2.4 0.9 %copy-start.4 = (bf16[2,128,256]{2,1,0:T(8,128)(2,1)S(1)}, bf16[2,128,256]{2,1,0:T(8,128)(2,1)}, u32[]{:S(2)}) copy-start(bf16[2,128,256]{2,1,0:T(8,128)(2,1)} %v_ref.3) | copy-start | bytes 393220
  3.3 0.9 %copy-start.5 = (bf16[2,128,256]{2,1,0:T(8,128)(2,1)S(1)}, bf16[2,128,256]{2,1,0:T(8,128)(2,1)}, u32[]{:S(2)}) copy-start(bf16[2,128,256]{2,1,0:T(8,128)(2,1)} %og_ref.1) | copy-start | bytes 393220
  4.2 33.3 %copy-start.6 = (bf16[2,128,256]{2,1,0:T(8,128)(2,1)S(1)}, bf16[2,128,256]{2,1,0:T(8,128)(2,1)}, u32[]{:S(2)}) copy-start(bf16[2,128,256]{2,1,0:T(8,128)(2,1)} %q_ref.1) | copy-start | bytes 393220
  35.5 1.0 %copy-start.1 = (bf16[8,2,128,256]{3,2,1,0:T(8,128)(2,1)}, bf16[8,2,128,256]{3,2,1,0:T(8,128)(2,1)S(1)}, u32[]{:S(2)}) copy-start(bf16[8,2,128,256]{3,2,1,0:T(8,128)(2,1)S(1)} %get-tuple-element.19.win_ref) | copy-start | bytes 3145732
  36.5 1.0 %copy-start.2 = (bf16[8,2,128,256]{3,2,1,0:T(8,128)(2,1)}, bf16[8,2,128,256]{3,2,1,0:T(8,128)(2,1)S(1)}, u32[]{:S(2)}) copy-start(bf16[8,2,128,256]{3,2,1,0:T(8,128)(2,1)S(1)} %get-tuple-element.20.full_ref) | copy-start | bytes 3145732
  37.5 1.2 %copy-start = (bf16[256,2048]{1,0:T(8,128)(2,1)S(1)}, bf16[256,2048]{1,0:T(8,128)(2,1)}, u32[]{:S(2)}) copy-start(bf16[256,2048]{1,0:T(8,128)(2,1)} %w_ref.1) | copy-start | bytes 3145732

commit v2 on v0

v2 whole, which is shorter than its diff:
```python
import functools
import math

import jax
import jax.numpy as jnp
from jax import lax
from jax.experimental import pallas as pl
from jax.experimental.pallas import tpu as pltpu
from jax.sharding import PartitionSpec as P

HD = 128
NEGATIVE = -1e30
RING = 8
ROW = 4
MESH = pl.DeviceIdType.MESH
VMEM = pltpu.VMEM
F32 = jnp.float32
BF16 = jnp.bfloat16

CORE_ORDER = (4, 3, -3, 2, -2, 1, -1, 0)
RING_ORDER = (-4, 4, -3, 3, -2, 2, -1, 1, 0)
SIDES = ((0, -1), (1, 1))
OWN, SIB, NEAR, CROSS, FAR, ODD = (0, 1), 2, (3, 4), (5, 6), (7, 8), 9
PAIRS = 10


def wrap(index, size):
    return lax.rem(index + size, size)


def dot_nn(a, b):
    return lax.dot_general(a, b, (((1,), (0,)), ((), ())), preferred_element_type=F32)


def dot_nt(a, b):
    return lax.dot_general(a, b, (((1,), (1,)), ((), ())), preferred_element_type=F32)


def dot_tn(a, b):
    return lax.dot_general(a, b, (((0,), (0,)), ((), ())), preferred_element_type=F32)


def listed_in(lists_ref, counts_ref, variant, row, block):
    count = counts_ref[variant, row]
    hit = jnp.int32(0)
    for slot in range(lists_ref.shape[0]):
        same = (lists_ref[slot, variant, row] == block) & (count > slot)
        hit = jnp.where(same, 1, hit)
    return hit


def greet(partners):
    barrier = pltpu.get_barrier_semaphore()
    for partner in partners:
        pl.semaphore_signal(barrier, inc=1, device_id=partner, device_id_type=MESH)
    pl.semaphore_wait(barrier, len(partners))


def ring_reduce(own, landed, send_sem, recv_sem, me, device_at):
    sides = ((0, -1), (1, 1))
    copies = {}

    def send(side, half, distance):
        step = sides[side][1]
        first = distance == (4 if side == half else 3)
        target = wrap(me + step * distance, RING)
        origin = own.at[target, half] if first else landed.at[side, half, distance]
        copy = pltpu.make_async_remote_copy(
            src_ref=origin,
            dst_ref=landed.at[side, half, distance - 1],
            send_sem=send_sem.at[side, half, distance - 1],
            recv_sem=recv_sem.at[side, half, distance - 1],
            device_id=device_at(wrap(me + step, RING)),
            device_id_type=MESH,
        )
        copy.start()
        copies[side, half, distance] = copy

    def begin():
        for half in range(2):
            for side in range(2):
                start = half if side == 0 else 1 - half
                send(side, start, 4 if side == start else 3)

    def advance(distance, side, half):
        if (side, half, distance) not in copies:
            return
        copies[side, half, distance].wait_recv()
        if distance > 1:
            target = wrap(me + sides[side][1] * (distance - 1), RING)
            here = landed.at[side, half, distance - 1]
            here[...] = (here[...].astype(F32) + own[target, half].astype(F32)).astype(BF16)
            send(side, half, distance - 1)

    def result(half):
        return (
            own[me, half].astype(F32)
            + landed[0, half, 0].astype(F32)
            + landed[1, half, 0].astype(F32)
        )

    def finish():
        for copy in copies.values():
            copy.wait_send()

    return begin, advance, result, finish


def whole_kernel(
    lists_ref, counts_ref, q_hbm, k_hbm, v_hbm, w_hbm, og_hbm,
    layer_ref, dq_ref, dk_ref, dv_ref, proj_out,
    q_ref, own_kv, w_ref, full, sib_kv, near, far, relay,
    grad_sum, grad, scores, prob_grads, attended,
    part, proj, layer_land, paired, pair_land, proj_land, row_out, row_land,
    own_term, term, sib_term, from_sib, from_far, relay_term, home_term,
    load_sem, ring_send, ring_recv, near_send, near_recv, sib_send, sib_recv, share_send, share_recv,
    far_send, far_recv, back_send, back_recv, home_send, home_recv,
    layer_send, layer_recv, pair_send, pair_recv, proj_send, proj_recv, row_send, row_recv,
):
    d = lax.axis_index("dp")
    t = lax.axis_index("tensor")
    n_dp = lax.axis_size("dp")
    core = lax.rem(d, 2)
    x = lax.rem(d // 2, ROW)
    y = d // (2 * ROW)
    scale = 1.0 / math.sqrt(HD)
    variants, rows, width = q_ref.shape
    heads = width // HD

    def at(yy, xx, cc):
        return ((yy * ROW + xx) * 2 + cc, t)

    def remote(src, dst, send, recv, device):
        copy = pltpu.make_async_remote_copy(
            src_ref=src, dst_ref=dst, send_sem=send, recv_sem=recv,
            device_id=device, device_id_type=MESH,
        )
        copy.start()
        return copy

    sib = d + 1 - 2 * core
    beside = [wrap(d - 2, n_dp), wrap(d + 2, n_dp)]
    odd = wrap(d + 2 * (2 * core - 1) + 1 - 2 * core, n_dp)
    odd_key = wrap(d + 2 * (1 - 2 * core), n_dp)
    odd_side = 1 - core

    loads = [
        pltpu.make_async_copy(k_hbm, own_kv.at[0], load_sem.at[0]),
        pltpu.make_async_copy(v_hbm, own_kv.at[1], load_sem.at[1]),
        pltpu.make_async_copy(q_hbm, q_ref, load_sem.at[2]),
        pltpu.make_async_copy(og_hbm, full.at[t], load_sem.at[3]),
        pltpu.make_async_copy(w_hbm, w_ref, load_sem.at[4]),
    ]
    for copy in loads:
        copy.start()
    greet(
        [(sib, t), (beside[0], t), (beside[1], t), (odd, t)]
        + [(d, wrap(t + s, RING)) for s in (-1, 1)]
        + [at(wrap(y + s, RING), x, core) for s in (-1, 1)]
        + [at(y, lax.rem(x + s, ROW), core) for s in range(1, ROW)]
    )

    hops = {}

    def hop(side, distance, half):
        step = SIDES[side][1]
        source = wrap(t - step * (distance - 1), RING)
        hops[side, distance, half] = remote(
            og_hbm.at[half] if distance == 1 else full.at[source, half],
            full.at[source, half],
            ring_send.at[side, distance - 1, half],
            ring_recv.at[side, distance - 1, half],
            (d, wrap(t + step, RING)),
        )

    def hop_on(distance):
        for half in range(2):
            for side in range(2):
                if (side, distance, half) in hops:
                    hops[side, distance, half].wait_recv()
                    if distance < 3 or (distance == 3 and half == side):
                        hop(side, distance + 1, half)

    for half in range(2):
        for side in range(2):
            hop(side, 1, half)

    near_copies, sib_copies, share_copies, far_copies = {}, {}, {}, {}
    for kv, source in enumerate((k_hbm, v_hbm)):
        for side in range(2):
            near_copies[1 - side, kv] = remote(
                source, near.at[1 - side, core, kv],
                near_send.at[1 - side, kv], near_recv.at[1 - side, kv], (beside[side], t),
            )
        sib_copies[kv] = remote(
            source, sib_kv.at[kv], sib_send.at[kv], sib_recv.at[kv], (sib, t)
        )

    relay_pick = [
        listed_in(lists_ref, counts_ref, 1, beside[1], beside[0]) == 1,
        listed_in(lists_ref, counts_ref, 1, beside[0], beside[1]) == 1,
        listed_in(lists_ref, counts_ref, 1, odd, odd_key) == 1,
    ]

    def pass_on(kv):
        for side in range(2):
            near_copies[side, kv].wait_recv()
            share_copies[side, kv] = remote(
                near.at[side, core, kv], near.at[side, core, kv],
                share_send.at[side, kv], share_recv.at[side, kv], (sib, t),
            )
            relay[side, kv] = jnp.where(
                relay_pick[side], near[side, core, kv, 1], near[side, core, kv, 0]
            )
            far_copies[side, kv] = remote(
                relay.at[side, kv], far.at[side, kv],
                far_send.at[side, kv], far_recv.at[side, kv], (beside[1 - side], t),
            )
        relay[2, kv] = jnp.where(
            relay_pick[2], near[odd_side, core, kv, 1], near[odd_side, core, kv, 0]
        )
        far_copies[2, kv] = remote(
            relay.at[2, kv], far.at[2, kv], far_send.at[2, kv], far_recv.at[2, kv], (odd, t)
        )

    offsets = {
        SIB: 1 - 2 * core, NEAR[0]: -2, NEAR[1]: 2, CROSS[0]: -1 - 2 * core,
        CROSS[1]: 3 - 2 * core, FAR[0]: -4, FAR[1]: 4, ODD: 6 * core - 3,
    }
    which, live = {}, {}
    for p, offset in offsets.items():
        first = listed_in(lists_ref, counts_ref, 0, d, d + offset)
        which[p] = listed_in(lists_ref, counts_ref, 1, d, d + offset)
        live[p] = (first + which[p]) > 0

    def cols(h):
        return slice(h * HD, (h + 1) * HD)

    def pair_kv(p, kv, h):
        if p in OWN:
            return own_kv[kv, p, :, cols(h)]
        if p == SIB:
            first, second = (sib_kv[kv, v, :, cols(h)] for v in range(2))
            return jnp.where(which[p] == 1, second, first)
        if p in NEAR or p in CROSS:
            side, holder = (p - NEAR[0], core) if p in NEAR else (p - CROSS[0], 1 - core)
            first, second = (near[side, holder, kv, v, :, cols(h)] for v in range(2))
            return jnp.where(which[p] == 1, second, first)
        return far[p - FAR[0], kv, :, cols(h)]

    def of_variant(p, ref, h):
        return ref[p if p in OWN else which[p], :, cols(h)]

    def pick(p, stats):
        return stats[p] if p in OWN else jnp.where(which[p] == 1, stats[1], stats[0])

    def merge(p, stats, new, combine, neutral):
        if p in OWN:
            stats[p] = combine(stats[p], new)
        else:
            for v in range(variants):
                stats[v] = combine(stats[v], jnp.where(which[p] == v, new, neutral))

    def per_head(shape, fill):
        return [[jnp.full(shape, fill, F32) for _ in range(variants)] for _ in range(heads)]

    tops = per_head((1, rows), NEGATIVE)

    def score(p):
        for h in range(heads):
            s = dot_nt(pair_kv(p, 0, h), of_variant(p, q_ref, h)) * scale
            if p not in OWN:
                s = jnp.where(live[p], s, NEGATIVE)
            scores[p, h] = s
            merge(p, tops[h], jnp.max(s, axis=0, keepdims=True), jnp.maximum, NEGATIVE)

    def grad_add(distance, first=False):
        sources = [t] if distance == 0 else [wrap(t - distance, RING)]
        if 0 < distance < 4:
            sources.append(wrap(t + distance, RING))
        for source in sources:
            columns = pl.ds(pl.multiple_of(source * width, width), width)
            piece = dot_nt(full[source].reshape(variants * rows, width), w_ref[:, columns])
            grad_sum[...] = piece if first else grad_sum[...] + piece

    for copy in loads:
        copy.wait()
    for p in OWN:
        score(p)
    grad_add(0, first=True)
    pass_on(0)
    hop_on(1)
    sib_copies[0].wait_recv()
    for p in (SIB, *NEAR):
        score(p)
    grad_add(1)
    pass_on(1)
    hop_on(2)
    for side in range(2):
        share_copies[side, 0].wait_recv()
    for p in CROSS:
        score(p)
    grad_add(2)
    hop_on(3)
    for j in range(3):
        far_copies[j, 0].wait_recv()
    for p in (*FAR, ODD):
        score(p)
    sums = per_head((1, rows), 0.0)
    for p in range(PAIRS):
        for h in range(heads):
            e = jnp.exp(scores[p, h] - pick(p, tops[h]))
            scores[p, h] = e
            merge(p, sums[h], jnp.sum(e, axis=0, keepdims=True), jnp.add, 0.0)
    inverse = [[1.0 / s for s in sums[h]] for h in range(heads)]
    sib_copies[1].wait_recv()
    for side in range(2):
        share_copies[side, 1].wait_recv()
    for j in range(3):
        far_copies[j, 1].wait_recv()
    for h in range(heads):
        outs = [jnp.zeros((rows, HD), F32) for _ in range(variants)]
        for p in range(PAIRS):
            prob = scores[p, h] * pick(p, inverse[h])
            scores[p, h] = prob
            merge(p, outs, dot_tn(prob.astype(BF16), pair_kv(p, 1, h)), jnp.add, 0.0)
        for v in range(variants):
            attended[v, :, cols(h)] = outs[v].astype(BF16)

    for r in RING_ORDER[1:]:
        target = wrap(t + r, RING)
        columns = pl.ds(pl.multiple_of(target * width, width), width)
        flat = attended[...].reshape(variants * rows, width)
        part[target] = dot_nn(flat, w_ref[:, columns]).astype(BF16).reshape(variants, rows, width)
    layer_begin, layer_advance, layer_result, layer_finish = ring_reduce(
        part, layer_land, layer_send, layer_recv, t, lambda z: (d, z)
    )
    layer_begin()

    hop_on(4)
    share = width // RING
    half_rows = paired.shape[2]
    swaps = []
    for j, r in enumerate(CORE_ORDER):
        chunk = wrap(y + r, RING)
        flat = attended[...].reshape(variants * rows, width)
        low = dot_tn(full[chunk].reshape(variants * rows, width), flat).astype(BF16)
        for b in range(RING):
            proj[b % 2, chunk, pl.ds((b // 2) * share, share)] = low[b * share:(b + 1) * share]
        swaps.append(remote(
            proj.at[1 - core, chunk], pair_land.at[chunk], pair_send.at[j], pair_recv.at[j], (sib, t)
        ))
    grad_add(3)
    grad_add(4)
    grad[...] = grad_sum[...].astype(BF16).reshape(variants, rows, width)

    back = {}

    def send_back(p, kv):
        if p == SIB:
            slot, target, device = 0, sib_term.at[kv], sib
        elif p in CROSS:
            side = p - CROSS[0]
            slot, target, device = 1 + side, from_sib.at[side, kv], sib
        elif p in FAR:
            side = p - FAR[0]
            slot, target, device = 3 + side, from_far.at[side, kv], beside[side]
        elif p == ODD:
            slot, target, device = 5, from_far.at[2, kv], odd
        else:
            return
        back[slot, kv] = remote(
            term.at[p - SIB, kv], target, back_send.at[slot, kv], back_recv.at[slot, kv], (device, t)
        )

    outward = (*FAR, ODD, *CROSS, SIB, *NEAR, *OWN)
    deltas = per_head((1, rows), 0.0)
    for p in outward:
        for h in range(heads):
            prob = scores[p, h]
            low = prob.astype(BF16)
            gradient = of_variant(p, grad, h)
            dp = dot_nt(pair_kv(p, 1, h), gradient)
            prob_grads[p, h] = dp
            merge(p, deltas[h], jnp.sum(prob * dp, axis=0, keepdims=True), jnp.add, 0.0)
            value = dot_nn(low, gradient)
            if p in OWN:
                own_term[1, p, :, cols(h)] = value
            else:
                term[p - SIB, 1, :, cols(h)] = value.astype(BF16)
        send_back(p, 1)

    def layer_step(distance):
        for half in range(2):
            for side in range(2):
                layer_advance(distance, side, half)

    def proj_step(distance):
        for half in range(2):
            for side in range(2):
                proj_advance(distance, side, half)

    layer_step(4)
    for j, r in enumerate(CORE_ORDER):
        chunk = wrap(y + r, RING)
        swaps[j].wait_recv()
        for half in range(2):
            span = pl.ds(half * half_rows, half_rows)
            both = proj[core, chunk, span].astype(F32) + pair_land[chunk, span].astype(F32)
            paired[chunk, half] = both.astype(BF16)
    proj_begin, proj_advance, proj_result, proj_finish = ring_reduce(
        paired, proj_land, proj_send, proj_recv, y, lambda yy: at(yy, x, core)
    )
    proj_begin()

    dqs = per_head((rows, HD), 0.0)
    for p in outward:
        for h in range(heads):
            ds = (scores[p, h] * (prob_grads[p, h] - pick(p, deltas[h])) * scale).astype(BF16)
            merge(p, dqs[h], dot_tn(ds, pair_kv(p, 0, h)), jnp.add, 0.0)
            value = dot_nn(ds, of_variant(p, q_ref, h))
            if p in OWN:
                own_term[0, p, :, cols(h)] = value
            else:
                term[p - SIB, 0, :, cols(h)] = value.astype(BF16)
        send_back(p, 0)
    for h in range(heads):
        for v in range(variants):
            dq_ref[v, :, cols(h)] = dqs[h][v].astype(BF16)

    home = {}
    sib_pick = [listed_in(lists_ref, counts_ref, 1, sib, b) == 1 for b in beside]
    own_pick = listed_in(lists_ref, counts_ref, 1, sib, d) == 1

    def relay_back(kv):
        for slot in range(1, 6):
            back[slot, kv].wait_recv()
        for side in range(2):
            parts = [
                (which[NEAR[side]] == 1, term[NEAR[side] - SIB, kv]),
                (sib_pick[side], from_sib[side, kv]),
                (relay_pick[side], from_far[side, kv]),
            ]
            extra = from_far[2, kv].astype(F32)
            extra = jnp.where(odd_side == side, extra, 0.0)
            both = [jnp.where(relay_pick[2], 0.0, extra), jnp.where(relay_pick[2], extra, 0.0)]
            for second, value in parts:
                value = value.astype(F32)
                both[0] = both[0] + jnp.where(second, 0.0, value)
                both[1] = both[1] + jnp.where(second, value, 0.0)
            for v in range(variants):
                relay_term[side, kv, v] = both[v].astype(BF16)
            home[side, kv] = remote(
                relay_term.at[side, kv], home_term.at[1 - side, kv],
                home_send.at[side, kv], home_recv.at[1 - side, kv], (beside[side], t),
            )

    relay_back(1)
    layer_step(3)
    proj_step(4)
    relay_back(0)
    proj_step(3)
    layer_step(2)
    proj_step(2)
    layer_step(1)
    proj_step(1)

    for half in range(2):
        piece = proj_result(half).astype(BF16)
        for i in range(half_rows // share):
            row_out[half * (half_rows // share) + i] = piece[i * share:(i + 1) * share]
    row_copies = []
    for s in range(1, ROW):
        xx = lax.rem(x + s, ROW)
        row_copies.append(remote(
            row_out.at[xx], row_land.at[s - 1], row_send.at[s - 1], row_recv.at[s - 1], at(y, xx, core)
        ))
    for half in range(2):
        layer_ref[half] = layer_result(half).astype(BF16)
    for kv, out in ((1, dv_ref), (0, dk_ref)):
        back[0, kv].wait_recv()
        for side in range(2):
            home[1 - side, kv].wait_recv()
        value = sib_term[kv].astype(F32)
        for v in range(variants):
            mine = jnp.where(own_pick, value if v == 1 else 0.0, 0.0 if v == 1 else value)
            total = own_term[kv, v] + mine
            for side in range(2):
                total = total + home_term[side, kv, v].astype(F32)
            out[v] = total.astype(BF16)
    total = row_out[x].astype(F32)
    for s in range(ROW - 1):
        row_copies[s].wait_recv()
        total = total + row_land[s].astype(F32)
    proj_out[...] = total

    for group in (hops, near_copies, sib_copies, share_copies, far_copies, back, home):
        for copy in group.values():
            copy.wait_send()
    for copy in swaps + row_copies:
        copy.wait_send()
    layer_finish()
    proj_finish()


def settle_kernel(*refs):
    count = len(refs) // 2
    for source, target in zip(refs[:count], refs[count:]):
        target[...] = source[...]


def local(queries, key_rows, value_rows, out_weight, out_grad, ibd_lists, ibd_counts):
    variants, rows, width = queries.shape
    heads = width // HD
    share = width // RING
    half_rows = ROW * share // 2
    smem = pl.BlockSpec(memory_space=pltpu.SMEM)
    vmem = pl.BlockSpec(memory_space=VMEM)
    anywhere = pl.BlockSpec(memory_space=pl.ANY)
    dma = pltpu.SemaphoreType.DMA
    block = (rows, width)
    outs = (
        jax.ShapeDtypeStruct((variants, *block), BF16),
        jax.ShapeDtypeStruct((variants, *block), BF16),
        jax.ShapeDtypeStruct((variants, *block), BF16),
        jax.ShapeDtypeStruct((variants, *block), BF16),
        jax.ShapeDtypeStruct((share, width), F32),
    )
    results = pl.pallas_call(
        whole_kernel,
        out_shape=outs,
        in_specs=[smem, smem] + [anywhere] * 5,
        out_specs=(vmem,) * 5,
        scratch_shapes=[
            VMEM((variants, *block), BF16),
            VMEM((2, variants, *block), BF16),
            VMEM(out_weight.shape, BF16),
            VMEM((RING, variants, *block), BF16),
            VMEM((2, variants, *block), BF16),
            VMEM((2, 2, 2, variants, *block), BF16),
            VMEM((3, 2, *block), BF16),
            VMEM((3, 2, *block), BF16),
            VMEM((variants * rows, width), F32),
            VMEM((variants, *block), BF16),
            VMEM((PAIRS, heads, rows, rows), F32),
            VMEM((PAIRS, heads, rows, rows), F32),
            VMEM((variants, *block), BF16),
            VMEM((RING, variants, *block), BF16),
            VMEM((2, RING, ROW * share, width), BF16),
            VMEM((2, 2, 4, *block), BF16),
            VMEM((RING, 2, half_rows, width), BF16),
            VMEM((RING, ROW * share, width), BF16),
            VMEM((2, 2, 4, half_rows, width), BF16),
            VMEM((ROW, share, width), BF16),
            VMEM((ROW - 1, share, width), BF16),
            VMEM((2, variants, *block), F32),
            VMEM((PAIRS - 2, 2, *block), BF16),
            VMEM((2, *block), BF16),
            VMEM((2, 2, *block), BF16),
            VMEM((3, 2, *block), BF16),
            VMEM((2, 2, variants, *block), BF16),
            VMEM((2, 2, variants, *block), BF16),
            dma((5,)),
            dma((2, 4, 2)), dma((2, 4, 2)),
            dma((2, 2)), dma((2, 2)), dma((2,)), dma((2,)), dma((2, 2)), dma((2, 2)),
            dma((3, 2)), dma((3, 2)), dma((6, 2)), dma((6, 2)), dma((2, 2)), dma((2, 2)),
            dma((2, 2, 4)), dma((2, 2, 4)), dma((8,)), dma((8,)),
            dma((2, 2, 4)), dma((2, 2, 4)), dma((ROW - 1,)), dma((ROW - 1,)),
        ],
        compiler_params=pltpu.CompilerParams(
            collective_id=0, has_side_effects=True, vmem_limit_bytes=60 * 1024 * 1024
        ),
        name="whole",
    )(
        jnp.transpose(ibd_lists, (2, 0, 1)), ibd_counts,
        queries, key_rows, value_rows, out_weight, out_grad,
    )
    return pl.pallas_call(
        settle_kernel,
        out_shape=outs,
        in_specs=[vmem] * 5,
        out_specs=(vmem,) * 5,
        name="settle",
    )(*results)


def solution(mesh):
    spec = P(None, "dp", "tensor")
    return jax.shard_map(
        local,
        mesh=mesh,
        in_specs=(spec, spec, spec, P("tensor", None), spec, P(), P()),
        out_specs=(spec, spec, spec, spec, P("dp", "tensor")),
        check_vma=False,
    )
```

time: 278 us -> 64.1 us (0.23); the launches traced: 273 us -> 63.2 us
  waiting for transfers between devices: 133 us -> 0 us
  Pallas kernels: 0 us -> 62.6 us
  starting transfers between devices: 60.7 us -> 0 us
  local copies, waits for them, and re-layouts: 39.5 us -> 0 us
  matrix products: 22.8 us -> 0 us
  between operations: 14.2 us -> 0.64 us
  other arithmetic: 3.09 us -> 0 us
    unnamed x4 -> x0, waiting for transfers between devices: 106 us -> none
    pallas_call x0 -> x2, Pallas kernels: none -> 62.6 us  [the longest x1 60.7 us: local(): pl.pallas_call(whole_kernel, out_shape=outs, in_specs=[smem, smem] + [any...]
    ppermute x16 -> x0, starting transfers between devices: 60.4 us -> none  [from_behind(): return lax.ppermute(block, axis, route)]
    dot_general x9 -> x0, matrix products: 22.8 us -> none  [the longest x1 5.12 us: local(): jnp.einsum('vhqk,vqhd->vkhd', score_grads, query_heads, preferred_element...]
    ppermute x16 -> x0, waiting for transfers between devices: 19.9 us -> none  [from_behind(): return lax.ppermute(block, axis, route)]
    transpose x2 -> x0, local copies, waits for them, and re-layouts: 12.7 us -> none  [the longest x1 7.78 us: local(): jnp.einsum('vhqk,vqhd->vkhd', score_grads, query_heads, preferred_element...]
    unnamed x32 -> x0, local copies, waits for them, and re-layouts: 11.9 us -> none
    another operation x5 -> x0, local copies, waits for them, and re-layouts: 10.2 us -> none  [the longest x3 8.48 us: local(): jnp.stack([key_terms, value_terms])]
  transfers between devices with their start and end apart: 19 -> 0, of which waited for: 5 -> 0; matrix products, arithmetic and copies ran while one was open for 22% -> 0% of each run, Pallas kernels for 0% -> 0%
where the time goes in v2:
time: 64.1 us; the launch traced here: 63.2 us
  Pallas kernels  62.6 us (98%)
    pallas_call x1, Pallas kernels, local(): pl.pallas_call(whole_kernel, out_shape=outs, in_specs=[smem, smem] + [any...  60.7 us
    pallas_call x1, Pallas kernels, local(): pl.pallas_call(settle_kernel, out_shape=outs, in_specs=[vmem] * 5, out_sp...  1.9 us

profile of v2, /device:TPU:1, one launch (start us, length us, event | category | flops | bytes accessed | tf_op | source)
XLA Modules:
  0.0 63.2 jit_solution(531281532409647801)
XLA Ops:
  0.6 60.7 %whole.1 = (bf16[2,128,256]{2,1,0:T(8,128)(2,1)}, bf16[2,128,256]{2,1,0:T(8,128)(2,1)}, bf16[2,128,256]{2,1,0:T(8,128)(2,1)}, bf16[2,128,256]{2,1,0:T(8,128)(2,1)}, f32[32,256]{1,0:T(8,128)}) custom-call(s32[9,2,64]{2,1,0:T(2,128)} %bitcast.1, s32[2,64]{1,0:T(2,128)} %counts_ref.1, bf16[2,128,256]{2,1,0:T(8,128)(2,1)} %q_hbm.1, bf16[2,128,256]{2,1,0:T(8,128)(2,1)} %k_hbm.1, ...), custom_call_target="tpu_custom_call" | custom-call | tf_op jit(solution)/shard_map/whole/pallas_call | solution.py:529
  61.3 1.9 %settle.1 = (bf16[2,128,256]{2,1,0:T(8,128)(2,1)}, bf16[2,128,256]{2,1,0:T(8,128)(2,1)}, bf16[2,128,256]{2,1,0:T(8,128)(2,1)}, bf16[2,128,256]{2,1,0:T(8,128)(2,1)}, f32[32,256]{1,0:T(8,128)}) custom-call(bf16[2,128,256]{2,1,0:T(8,128)(2,1)} %get-tuple-element.10.refs_0_, bf16[2,128,256]{2,1,0:T(8,128)(2,1)} %get-tuple-element.11.refs_1_, ...), custom_call_target="tpu_custom_call" | custom-call | tf_op jit(solution)/shard_map/settle/pallas_call | solution.py:578

commit v3 on v2

--- a/solution.py
+++ b/solution.py
@@ -18,7 +18,6 @@
 BF16 = jnp.bfloat16
 
 CORE_ORDER = (4, 3, -3, 2, -2, 1, -1, 0)
-RING_ORDER = (-4, 4, -3, 3, -2, 2, -1, 1, 0)
 SIDES = ((0, -1), (1, 1))
 OWN, SIB, NEAR, CROSS, FAR, ODD = (0, 1), 2, (3, 4), (5, 6), (7, 8), 9
 PAIRS = 10
@@ -76,11 +75,9 @@
         copy.start()
         copies[side, half, distance] = copy
 
-    def begin():
-        for half in range(2):
-            for side in range(2):
-                start = half if side == 0 else 1 - half
-                send(side, start, 4 if side == start else 3)
+    def begin(distance):
+        for side in range(2):
+            send(side, side if distance == 4 else 1 - side, distance)
 
     def advance(distance, side, half):
         if (side, half, distance) not in copies:
@@ -302,6 +299,7 @@
         score(p)
     grad_add(2)
     hop_on(3)
+    grad_add(3)
     for j in range(3):
         far_copies[j, 0].wait_recv()
     for p in (*FAR, ODD):
@@ -327,30 +325,53 @@
         for v in range(variants):
             attended[v, :, cols(h)] = outs[v].astype(BF16)
 
-    for r in RING_ORDER[1:]:
+    layer_begin, layer_advance, layer_result, layer_finish = ring_reduce(
+        part, layer_land, layer_send, layer_recv, t, lambda z: (d, z)
+    )
+    for r in CORE_ORDER:
         target = wrap(t + r, RING)
         columns = pl.ds(pl.multiple_of(target * width, width), width)
         flat = attended[...].reshape(variants * rows, width)
         part[target] = dot_nn(flat, w_ref[:, columns]).astype(BF16).reshape(variants, rows, width)
-    layer_begin, layer_advance, layer_result, layer_finish = ring_reduce(
-        part, layer_land, layer_send, layer_recv, t, lambda z: (d, z)
-    )
-    layer_begin()
+        if r in (4, -3):
+            layer_begin(abs(r))
 
     hop_on(4)
     share = width // RING
     half_rows = paired.shape[2]
-    swaps = []
+    swaps = {}
     for j, r in enumerate(CORE_ORDER):
         chunk = wrap(y + r, RING)
         flat = attended[...].reshape(variants * rows, width)
         low = dot_tn(full[chunk].reshape(variants * rows, width), flat).astype(BF16)
         for b in range(RING):
             proj[b % 2, chunk, pl.ds((b // 2) * share, share)] = low[b * share:(b + 1) * share]
-        swaps.append(remote(
+        swaps[r] = remote(
             proj.at[1 - core, chunk], pair_land.at[chunk], pair_send.at[j], pair_recv.at[j], (sib, t)
-        ))
-    grad_add(3)
+        )
+    proj_begin, proj_advance, proj_result, proj_finish = ring_reduce(
+        paired, proj_land, proj_send, proj_recv, y, lambda yy: at(yy, x, core)
+    )
+
+    def pair_up(*chunks):
+        for r in chunks:
+            chunk = wrap(y + r, RING)
+            swaps[r].wait_recv()
+            for half in range(2):
+                span = pl.ds(half * half_rows, half_rows)
+                both = proj[core, chunk, span].astype(F32) + pair_land[chunk, span].astype(F32)
+                paired[chunk, half] = both.astype(BF16)
+
+    def layer_step(distance):
+        for half in range(2):
+            for side in range(2):
+                layer_advance(distance, side, half)
+
+    def proj_step(distance):
+        for half in range(2):
+            for side in range(2):
+                proj_advance(distance, side, half)
+
     grad_add(4)
     grad[...] = grad_sum[...].astype(BF16).reshape(variants, rows, width)
 
@@ -373,60 +394,37 @@
             term.at[p - SIB, kv], target, back_send.at[slot, kv], back_recv.at[slot, kv], (device, t)
         )
 
-    outward = (*FAR, ODD, *CROSS, SIB, *NEAR, *OWN)
     deltas = per_head((1, rows), 0.0)
-    for p in outward:
-        for h in range(heads):
-            prob = scores[p, h]
-            low = prob.astype(BF16)
-            gradient = of_variant(p, grad, h)
-            dp = dot_nt(pair_kv(p, 1, h), gradient)
-            prob_grads[p, h] = dp
-            merge(p, deltas[h], jnp.sum(prob * dp, axis=0, keepdims=True), jnp.add, 0.0)
-            value = dot_nn(low, gradient)
-            if p in OWN:
-                own_term[1, p, :, cols(h)] = value
-            else:
-                term[p - SIB, 1, :, cols(h)] = value.astype(BF16)
-        send_back(p, 1)
-
-    def layer_step(distance):
-        for half in range(2):
-            for side in range(2):
-                layer_advance(distance, side, half)
-
-    def proj_step(distance):
-        for half in range(2):
-            for side in range(2):
-                proj_advance(distance, side, half)
-
-    layer_step(4)
-    for j, r in enumerate(CORE_ORDER):
-        chunk = wrap(y + r, RING)
-        swaps[j].wait_recv()
-        for half in range(2):
-            span = pl.ds(half * half_rows, half_rows)
-            both = proj[core, chunk, span].astype(F32) + pair_land[chunk, span].astype(F32)
-            paired[chunk, half] = both.astype(BF16)
-    proj_begin, proj_advance, proj_result, proj_finish = ring_reduce(
-        paired, proj_land, proj_send, proj_recv, y, lambda yy: at(yy, x, core)
-    )
-    proj_begin()
+
+    def value_terms(*which_pairs):
+        for p in which_pairs:
+            for h in range(heads):
+                prob = scores[p, h]
+                low = prob.astype(BF16)
+                gradient = of_variant(p, grad, h)
+                dp = dot_nt(pair_kv(p, 1, h), gradient)
+                prob_grads[p, h] = dp
+                merge(p, deltas[h], jnp.sum(prob * dp, axis=0, keepdims=True), jnp.add, 0.0)
+                value = dot_nn(low, gradient)
+                if p in OWN:
+                    own_term[1, p, :, cols(h)] = value
+                else:
+                    term[p - SIB, 1, :, cols(h)] = value.astype(BF16)
+            send_back(p, 1)
 
     dqs = per_head((rows, HD), 0.0)
-    for p in outward:
-        for h in range(heads):
-            ds = (scores[p, h] * (prob_grads[p, h] - pick(p, deltas[h])) * scale).astype(BF16)
-            merge(p, dqs[h], dot_tn(ds, pair_kv(p, 0, h)), jnp.add, 0.0)
-            value = dot_nn(ds, of_variant(p, q_ref, h))
-            if p in OWN:
-                own_term[0, p, :, cols(h)] = value
-            else:
-                term[p - SIB, 0, :, cols(h)] = value.astype(BF16)
-        send_back(p, 0)
-    for h in range(heads):
-        for v in range(variants):
-            dq_ref[v, :, cols(h)] = dqs[h][v].astype(BF16)
+
+    def key_terms(*which_pairs):
+        for p in which_pairs:
+            for h in range(heads):
+                ds = (scores[p, h] * (prob_grads[p, h] - pick(p, deltas[h])) * scale).astype(BF16)
+                merge(p, dqs[h], dot_tn(ds, pair_kv(p, 0, h)), jnp.add, 0.0)
+                value = dot_nn(ds, of_variant(p, q_ref, h))
+                if p in OWN:
+                    own_term[0, p, :, cols(h)] = value
+                else:
+                    term[p - SIB, 0, :, cols(h)] = value.astype(BF16)
+            send_back(p, 0)
 
     home = {}
     sib_pick = [listed_in(lists_ref, counts_ref, 1, sib, b) == 1 for b in beside]
@@ -455,14 +453,27 @@
                 home_send.at[side, kv], home_recv.at[1 - side, kv], (beside[side], t),
             )
 
+    value_terms(*FAR, ODD, *CROSS)
+    pair_up(4)
+    proj_begin(4)
+    pair_up(3, -3)
+    proj_begin(3)
+    value_terms(SIB, *NEAR, *OWN)
+    layer_step(4)
+    key_terms(*FAR, ODD, *CROSS)
+    pair_up(2, -2)
+    proj_step(4)
     relay_back(1)
+    pair_up(1, -1, 0)
+    proj_step(3)
     layer_step(3)
-    proj_step(4)
+    key_terms(SIB, *NEAR, *OWN)
+    for h in range(heads):
+        for v in range(variants):
+            dq_ref[v, :, cols(h)] = dqs[h][v].astype(BF16)
     relay_back(0)
-    proj_step(3)
+    proj_step(2)
     layer_step(2)
-    proj_step(2)
-    layer_step(1)
     proj_step(1)
 
     for half in range(2):
@@ -475,6 +486,7 @@
         row_copies.append(remote(
             row_out.at[xx], row_land.at[s - 1], row_send.at[s - 1], row_recv.at[s - 1], at(y, xx, core)
         ))
+    layer_step(1)
     for half in range(2):
         layer_ref[half] = layer_result(half).astype(BF16)
     for kv, out in ((1, dv_ref), (0, dk_ref)):
@@ -497,7 +509,7 @@
     for group in (hops, near_copies, sib_copies, share_copies, far_copies, back, home):
         for copy in group.values():
             copy.wait_send()
-    for copy in swaps + row_copies:
+    for copy in [*swaps.values(), *row_copies]:
         copy.wait_send()
     layer_finish()
     proj_finish()

time: 64.1 us -> 61.9 us (0.966)
  Pallas kernels: 62.6 us -> 61 us
    pallas_call x1, Pallas kernels: 60.7 us -> 59.1 us  [local(): pl.pallas_call(whole_kernel, out_shape=outs, in_specs=[smem, smem] + [any...]
where the time goes in v3:
time: 61.9 us; the launch traced here: 61.7 us
  Pallas kernels  61 us (99%)
  between operations  0.64 us (1%)
    pallas_call x1, Pallas kernels, local(): pl.pallas_call(whole_kernel, out_shape=outs, in_specs=[smem, smem] + [any...  59.1 us
    pallas_call x1, Pallas kernels, local(): pl.pallas_call(settle_kernel, out_shape=outs, in_specs=[vmem] * 5, out_sp...  1.9 us

profile of v3, /device:TPU:1, one launch (start us, length us, event | category | flops | bytes accessed | tf_op | source)
XLA Modules:
  0.0 61.7 jit_solution(3956867526788634040)
XLA Ops:
  0.6 59.1 %whole.1 = (bf16[2,128,256]{2,1,0:T(8,128)(2,1)}, bf16[2,128,256]{2,1,0:T(8,128)(2,1)}, bf16[2,128,256]{2,1,0:T(8,128)(2,1)}, bf16[2,128,256]{2,1,0:T(8,128)(2,1)}, f32[32,256]{1,0:T(8,128)}) custom-call(s32[9,2,64]{2,1,0:T(2,128)} %bitcast.1, s32[2,64]{1,0:T(2,128)} %counts_ref.1, bf16[2,128,256]{2,1,0:T(8,128)(2,1)} %q_hbm.1, bf16[2,128,256]{2,1,0:T(8,128)(2,1)} %k_hbm.1, ...), custom_call_target="tpu_custom_call" | custom-call | tf_op jit(solution)/shard_map/whole/pallas_call | solution.py:541
  59.8 1.9 %settle.1 = (bf16[2,128,256]{2,1,0:T(8,128)(2,1)}, bf16[2,128,256]{2,1,0:T(8,128)(2,1)}, bf16[2,128,256]{2,1,0:T(8,128)(2,1)}, bf16[2,128,256]{2,1,0:T(8,128)(2,1)}, f32[32,256]{1,0:T(8,128)}) custom-call(bf16[2,128,256]{2,1,0:T(8,128)(2,1)} %get-tuple-element.10.refs_0_, bf16[2,128,256]{2,1,0:T(8,128)(2,1)} %get-tuple-element.11.refs_1_, ...), custom_call_target="tpu_custom_call" | custom-call | tf_op jit(solution)/shard_map/settle/pallas_call | solution.py:590

commit v4 on v3

--- a/solution.py
+++ b/solution.py
@@ -170,8 +170,8 @@
             (d, wrap(t + step, RING)),
         )
 
-    def hop_on(distance):
-        for half in range(2):
+    def hop_on(distance, *halves):
+        for half in halves:
             for side in range(2):
                 if (side, distance, half) in hops:
                     hops[side, distance, half].wait_recv()
@@ -285,31 +285,34 @@
     for p in OWN:
         score(p)
     grad_add(0, first=True)
+    hop_on(1, 0)
     pass_on(0)
-    hop_on(1)
+    hop_on(1, 1)
     sib_copies[0].wait_recv()
     for p in (SIB, *NEAR):
         score(p)
     grad_add(1)
+    hop_on(2, 0)
     pass_on(1)
-    hop_on(2)
+    hop_on(2, 1)
     for side in range(2):
         share_copies[side, 0].wait_recv()
     for p in CROSS:
         score(p)
     grad_add(2)
-    hop_on(3)
-    grad_add(3)
+    hop_on(3, 0)
     for j in range(3):
         far_copies[j, 0].wait_recv()
     for p in (*FAR, ODD):
         score(p)
+    hop_on(3, 1)
     sums = per_head((1, rows), 0.0)
     for p in range(PAIRS):
         for h in range(heads):
             e = jnp.exp(scores[p, h] - pick(p, tops[h]))
             scores[p, h] = e
             merge(p, sums[h], jnp.sum(e, axis=0, keepdims=True), jnp.add, 0.0)
+    grad_add(3)
     inverse = [[1.0 / s for s in sums[h]] for h in range(heads)]
     sib_copies[1].wait_recv()
     for side in range(2):
@@ -325,18 +328,7 @@
         for v in range(variants):
             attended[v, :, cols(h)] = outs[v].astype(BF16)
 
-    layer_begin, layer_advance, layer_result, layer_finish = ring_reduce(
-        part, layer_land, layer_send, layer_recv, t, lambda z: (d, z)
-    )
-    for r in CORE_ORDER:
-        target = wrap(t + r, RING)
-        columns = pl.ds(pl.multiple_of(target * width, width), width)
-        flat = attended[...].reshape(variants * rows, width)
-        part[target] = dot_nn(flat, w_ref[:, columns]).astype(BF16).reshape(variants, rows, width)
-        if r in (4, -3):
-            layer_begin(abs(r))
-
-    hop_on(4)
+    hop_on(4, 0, 1)
     share = width // RING
     half_rows = paired.shape[2]
     swaps = {}
@@ -351,6 +343,10 @@
         )
     proj_begin, proj_advance, proj_result, proj_finish = ring_reduce(
         paired, proj_land, proj_send, proj_recv, y, lambda yy: at(yy, x, core)
+    )
+
+    layer_begin, layer_advance, layer_result, layer_finish = ring_reduce(
+        part, layer_land, layer_send, layer_recv, t, lambda z: (d, z)
     )
 
     def pair_up(*chunks):
@@ -453,28 +449,34 @@
                 home_send.at[side, kv], home_recv.at[1 - side, kv], (beside[side], t),
             )
 
-    value_terms(*FAR, ODD, *CROSS)
+    value_terms(*FAR, ODD)
+    for r in CORE_ORDER:
+        target = wrap(t + r, RING)
+        columns = pl.ds(pl.multiple_of(target * width, width), width)
+        flat = attended[...].reshape(variants * rows, width)
+        part[target] = dot_nn(flat, w_ref[:, columns]).astype(BF16).reshape(variants, rows, width)
+        if r in (4, -3):
+            layer_begin(abs(r))
     pair_up(4)
     proj_begin(4)
     pair_up(3, -3)
     proj_begin(3)
-    value_terms(SIB, *NEAR, *OWN)
-    layer_step(4)
-    key_terms(*FAR, ODD, *CROSS)
+    value_terms(*CROSS, SIB, *NEAR, *OWN)
+    key_terms(*FAR, ODD, *CROSS, SIB, *NEAR, *OWN)
     pair_up(2, -2)
     proj_step(4)
+    pair_up(1, -1, 0)
+    layer_step(4)
+    proj_step(3)
     relay_back(1)
-    pair_up(1, -1, 0)
-    proj_step(3)
     layer_step(3)
-    key_terms(SIB, *NEAR, *OWN)
+    proj_step(2)
+    relay_back(0)
+    layer_step(2)
+    proj_step(1)
     for h in range(heads):
         for v in range(variants):
             dq_ref[v, :, cols(h)] = dqs[h][v].astype(BF16)
-    relay_back(0)
-    proj_step(2)
-    layer_step(2)
-    proj_step(1)
 
     for half in range(2):
         piece = proj_result(half).astype(BF16)

time: 61.9 us -> 59.3 us (0.958)
  the two profiles are of different devices: /device:TPU:1 before, /device:TPU:8 now
where the time goes in v4:
time: 59.3 us; the launch traced here: 59.1 us
  Pallas kernels  58.4 us (98%)
  between operations  0.64 us (1%)
    pallas_call x1, Pallas kernels, local(): pl.pallas_call(whole_kernel, out_shape=outs, in_specs=[smem, smem] + [any...  56.5 us
    pallas_call x1, Pallas kernels, local(): pl.pallas_call(settle_kernel, out_shape=outs, in_specs=[vmem] * 5, out_sp...  1.9 us

profile of v4, /device:TPU:8, one launch (start us, length us, event | category | flops | bytes accessed | tf_op | source)
XLA Modules:
  0.0 59.1 jit_solution(6172657648570230825)
XLA Ops:
  0.6 56.5 %whole.1 = (bf16[2,128,256]{2,1,0:T(8,128)(2,1)}, bf16[2,128,256]{2,1,0:T(8,128)(2,1)}, bf16[2,128,256]{2,1,0:T(8,128)(2,1)}, bf16[2,128,256]{2,1,0:T(8,128)(2,1)}, f32[32,256]{1,0:T(8,128)}) custom-call(s32[9,2,64]{2,1,0:T(2,128)} %bitcast.1, s32[2,64]{1,0:T(2,128)} %counts_ref.1, bf16[2,128,256]{2,1,0:T(8,128)(2,1)} %q_hbm.1, bf16[2,128,256]{2,1,0:T(8,128)(2,1)} %k_hbm.1, ...), custom_call_target="tpu_custom_call" | custom-call | tf_op jit(solution)/shard_map/whole/pallas_call | solution.py:543
  57.2 1.9 %settle.1 = (bf16[2,128,256]{2,1,0:T(8,128)(2,1)}, bf16[2,128,256]{2,1,0:T(8,128)(2,1)}, bf16[2,128,256]{2,1,0:T(8,128)(2,1)}, bf16[2,128,256]{2,1,0:T(8,128)(2,1)}, f32[32,256]{1,0:T(8,128)}) custom-call(bf16[2,128,256]{2,1,0:T(8,128)(2,1)} %get-tuple-element.10.refs_0_, bf16[2,128,256]{2,1,0:T(8,128)(2,1)} %get-tuple-element.11.refs_1_, ...), custom_call_target="tpu_custom_call" | custom-call | tf_op jit(solution)/shard_map/settle/pallas_call | solution.py:592
